TPU v7x, 32 devices: a whole 2x2x4 slice. The times are simulated.
32 devices in a mesh: seg: 8 (over y, x, core), blk: 4 (over z).
Axes of the slice: x: 2, y: 2, z: 4, core: 2. Of those that a mesh axis runs over, the one named last changes fastest.
Arguments:
- two_site: float32 [8, 4, 128, 128], P('seg', 'blk'), may hold values from -6 to 6
- diag_left: float32 [8, 4, 2, 128, 128], P('seg', 'blk')
- diag_right: float32 [8, 4, 2, 128, 128], P('seg', 'blk')
- hop_left: float32 [8, 4, 16, 128, 128], P('seg', 'blk'), may hold values from -0.125 to 0.125
- hop_right: float32 [8, 4, 16, 128, 128], P('seg', 'blk'), may hold values from -0.125 to 0.125
- sector_sizes: int32 [8, 4], P('seg', 'blk'), may hold values from 1 to 128, 384 in all within a row
- ranks: int32 [8, 4], P('seg', 'blk'), may hold values from 1 to 128
Outputs:
- new_state: float32 [8, 4, 128, 128], P('seg', 'blk')
- left_boundary: float32 [8, 4, 18, 128, 128], P('seg', 'blk')
- right_boundary: float32 [8, 4, 18, 128, 128], P('seg', 'blk')
- energy: float32 [8], P('seg')
Inputs may be any that keep to these rules, and one draw needn't show every extreme that they name: Each row of sector_sizes sums to 384; the largest entry of every row is 128.
All inputs are finite; a program needn't handle non-finite values. No bound on the sum of `sector_sizes` on one device may be relied on, other than what follows from the above.
Results may differ from a plain program's by a relative error of at most 0.0003.
Values sent between devices are 32-bit elements; how exact they have to be, the bound alone decides.
A program may use at most 64 MiB of HBM per device.

v0:
```python
import jax
import jax.numpy as jnp
from jax import lax
from jax.sharding import PartitionSpec as P

ITERS = 4


highest = lax.Precision.HIGHEST
spectral_shift = 20.0


def padded_2(block, sides, width):
    for axis, dim in sides:
        count = lax.axis_size(axis)
        forward = [(i, i + 1) for i in range(count - 1)]
        backward = [(target, source) for source, target in forward]
        low = lax.ppermute(
            lax.slice_in_dim(block, block.shape[dim] - width, None, axis=dim), axis, forward
        )
        high = lax.ppermute(lax.slice_in_dim(block, 0, width, axis=dim), axis, backward)
        block = jnp.concatenate([low, block, high], axis=dim)
    return block


def passed_along(value, axis, steps):
    count = lax.axis_size(axis)
    leading, last = (max(0, -steps), min(count, count - steps))
    return lax.ppermute(value, axis, [(source, source + steps) for source in range(leading, last)])


def channel_apply(left_ops, vector, right_ops):
    halfway = jnp.einsum("qwij,qjk->qwik", left_ops, vector, precision=highest)
    return jnp.einsum("qwik,qwlk->qil", halfway, right_ops, precision=highest)


def channel_adjoint(left_ops, vector, right_ops):
    halfway = jnp.einsum("qwji,qjk->qwik", left_ops, vector, precision=highest)
    return jnp.einsum("qwik,qwkl->qil", halfway, right_ops, precision=highest)


def left_extend(kept_state, left_ops):
    halfway = jnp.einsum("qwij,qjl->qwil", left_ops, kept_state, precision=highest)
    return jnp.einsum("qik,qwil->qwkl", kept_state, halfway, precision=highest)


def right_extend(kept_state, right_ops):
    halfway = jnp.einsum("qik,qwlk->qwil", kept_state, right_ops, precision=highest)
    return jnp.einsum("qwil,qjl->qwij", halfway, kept_state, precision=highest)


def shards(two_site, diag_left, diag_right, hop_left, hop_right, sector_sizes, ranks):
    block_size = two_site.shape[2]
    positions = jnp.arange(block_size, dtype=jnp.int32)
    sector_size = sector_sizes[0]
    row_live = (positions[None, :] < sector_size[:, None]).astype(jnp.float32)
    live_mask = row_live[:, :, None] * row_live[:, None, :]
    keep_left = diag_left[0]
    keep_right = diag_right[0]
    raise_left = hop_left[0]
    raise_right = hop_right[0]
    vector = live_mask * two_site[0]
    last_vector = vector
    last_applied = vector
    for iteration in range(ITERS):
        own_terms = channel_apply(keep_left, vector, keep_right)
        carried = channel_adjoint(raise_left, vector, raise_right)
        stacked = jnp.stack([vector, carried], 0)
        padded = padded_2(stacked, (("blk", 1),), 1)
        previous = padded[0, :-2]
        following = padded[1, 2:]
        applied = live_mask * (
            own_terms + channel_apply(raise_left, previous, raise_right) + following
        )
        last_vector = vector
        last_applied = applied
        vector = spectral_shift * vector - applied
    quotient_top, quotient_low, final_sq, bond_total = lax.psum(
        (
            jnp.sum(last_vector * last_applied),
            jnp.sum(last_vector * last_vector),
            jnp.sum(vector * vector),
            jnp.sum(sector_size).astype(jnp.float32),
        ),
        "blk",
    )
    energy = quotient_top / quotient_low
    new_state = vector * jnp.sqrt(bond_total * block_size / final_sq)
    kept_count = jnp.minimum(ranks[0], sector_size)
    col_live = (positions[None, :] < kept_count[:, None]).astype(jnp.float32)
    kept_state = new_state * col_live[:, None, :]
    scale = 1.0 / jnp.sqrt(jnp.float32(block_size))
    new_left = (
        jnp.concatenate(
            [left_extend(kept_state, keep_left), left_extend(kept_state, raise_left)], 1
        )
        * scale
    )
    new_right = (
        jnp.concatenate(
            [right_extend(kept_state, keep_right), right_extend(kept_state, raise_right)], 1
        )
        * scale
    )
    left_boundary = passed_along(new_left, "seg", 1)
    right_boundary = passed_along(new_right, "seg", -1)
    return (new_state[None], left_boundary[None], right_boundary[None], jnp.reshape(energy, (1,)))


def solution(mesh):
    return jax.shard_map(
        shards,
        mesh=mesh,
        in_specs=(
            P("seg", "blk", None, None),
            P("seg", "blk", None, None, None),
            P("seg", "blk", None, None, None),
            P("seg", "blk", None, None, None),
            P("seg", "blk", None, None, None),
            P("seg", "blk"),
            P("seg", "blk"),
        ),
        out_specs=(
            P("seg", "blk", None, None),
            P("seg", "blk", None, None, None),
            P("seg", "blk", None, None, None),
            P("seg"),
        ),
        check_vma=False,
    )
```

profile of v0, /device:TPU:1, one launch (start us, length us, event | category | flops | bytes accessed | tf_op | source)
XLA Modules:
  0.0 115.8 jit_solution(636481537434978059)
XLA Ops:
  0.6 0.0 copy-start
  0.6 0.0 copy-start.1
  1.5 0.9 multiply_multiply_fusion.5
  2.4 1.8 %convolution_bitcast_fusion.11 = f32[16,128,128]{2,1,0:T(8,128)S(1)} fusion(f32[1,1,16,128,128]{4,3,2,1,0:T(8,128)S(1)} %copy-done, f32[1,1,128,128]{3,2,1,0:T(8,128)S(1)} %multiply_multiply_fusion.5), kind=kOutput, calls=%fused_computation.11 | convolution fusion | flops 402653184 | bytes 2162688 | tf_op jit(solution)/shard_map/qwji,qjk->qwik/dot_general | solution.py:38
  4.2 0.0 copy-start.2
  4.2 1.1 convolution_bitcast_fusion.30
  5.4 1.3 %collective-permute-start.1 = (f32[2,1,128,128]{3,2,1,0:T(8,128)S(1)}, f32[2,1,128,128]{3,2,1,0:T(8,128)S(1)}, u32[]{:S(2)}, u32[]{:S(2)}) collective-permute-start(f32[2,1,128,128]{3,2,1,0:T(8,128)S(1)} %pad_maximum_fusion), channel_id=1, source_target_pairs={{1,0},{2,1},{3,2},{5,4},{6,5},{7,6},{9,8},{10,9},{11,10},{13,12},{... | collective-permute-start | bytes 393224 | tf_op jit(solution)/shard_map/ppermute | solution.py:21
  6.7 4.7 %collective-permute-start = (f32[2,1,128,128]{3,2,1,0:T(8,128)S(1)}, f32[2,1,128,128]{3,2,1,0:T(8,128)S(1)}, u32[]{:S(2)}, u32[]{:S(2)}) collective-permute-start(f32[2,1,128,128]{3,2,1,0:T(8,128)S(1)} %pad_maximum_fusion), channel_id=1, source_target_pairs={{0,1},{1,2},{2,3},{4,5},{5,6},{6,7},{8,9},{9,10},{10,11},{12,13},{... | collective-permute-start | bytes 393224 | tf_op jit(solution)/shard_map/ppermute | solution.py:18
  11.4 0.3 convolution_bitcast_fusion.19
  12.3 1.2 %collective-permute-done = f32[2,1,128,128]{3,2,1,0:T(8,128)S(1)} collective-permute-done((f32[2,1,128,128]{3,2,1,0:T(8,128)S(1)}, f32[2,1,128,128]{3,2,1,0:T(8,128)S(1)}, u32[]{:S(2)}, u32[]{:S(2)}) %collective-permute-start) | collective-permute-done | bytes 131104 | tf_op jit(solution)/shard_map/ppermute | solution.py:18
  13.5 1.0 convolution_bitcast_fusion.10
  14.5 0.0 copy-start.3
  14.5 0.0 copy-start.4
  14.5 1.0 convolution_bitcast_fusion.29
  15.5 0.0 collective-permute-done.1
  15.5 0.3 fusion.33
  15.8 1.8 %convolution_bitcast_fusion.9 = f32[16,128,128]{2,1,0:T(8,128)S(1)} fusion(f32[1,1,16,128,128]{4,3,2,1,0:T(8,128)S(1)} %copy-done, f32[128,128]{1,0:T(8,128)S(1)} %fusion.33), kind=kOutput, calls=%fused_computation.9 | convolution fusion | flops 402653184 | bytes 2162688 | tf_op jit(solution)/shard_map/qwji,qjk->qwik/dot_general | solution.py:38
  17.6 1.1 convolution_bitcast_fusion.27
  18.8 1.3 %collective-permute-start.3 = (f32[2,1,128,128]{3,2,1,0:T(8,128)S(1)}, f32[2,1,128,128]{3,2,1,0:T(8,128)S(1)}, u32[]{:S(2)}, u32[]{:S(2)}) collective-permute-start(f32[2,1,128,128]{3,2,1,0:T(8,128)S(1)} %pad_maximum_fusion.1), channel_id=1, source_target_pairs={{1,0},{2,1},{3,2},{5,4},{6,5},{7,6},{9,8},{10,9},{11,10},{13,12},{... | collective-permute-start | bytes 393224 | tf_op jit(solution)/shard_map/ppermute | solution.py:21
  20.1 4.9 %collective-permute-start.2 = (f32[2,1,128,128]{3,2,1,0:T(8,128)S(1)}, f32[2,1,128,128]{3,2,1,0:T(8,128)S(1)}, u32[]{:S(2)}, u32[]{:S(2)}) collective-permute-start(f32[2,1,128,128]{3,2,1,0:T(8,128)S(1)} %pad_maximum_fusion.1), channel_id=1, source_target_pairs={{0,1},{1,2},{2,3},{4,5},{5,6},{6,7},{8,9},{9,10},{10,11},{12,13},{... | collective-permute-start | bytes 393224 | tf_op jit(solution)/shard_map/ppermute | solution.py:18
  25.0 0.3 convolution_bitcast_fusion.18
  25.3 1.5 %collective-permute-done.2 = f32[2,1,128,128]{3,2,1,0:T(8,128)S(1)} collective-permute-done((f32[2,1,128,128]{3,2,1,0:T(8,128)S(1)}, f32[2,1,128,128]{3,2,1,0:T(8,128)S(1)}, u32[]{:S(2)}, u32[]{:S(2)}) %collective-permute-start.2) | collective-permute-done | bytes 131104 | tf_op jit(solution)/shard_map/ppermute | solution.py:18
  26.8 1.0 convolution_bitcast_fusion.8
  27.8 1.0 convolution_bitcast_fusion.26
  28.8 0.0 collective-permute-done.3
  28.8 0.3 fusion.34
  29.1 1.8 %convolution_bitcast_fusion.7 = f32[16,128,128]{2,1,0:T(8,128)S(1)} fusion(f32[1,1,16,128,128]{4,3,2,1,0:T(8,128)S(1)} %copy-done, f32[128,128]{1,0:T(8,128)S(1)} %fusion.34), kind=kOutput, calls=%fused_computation.7 | convolution fusion | flops 402653184 | bytes 2162688 | tf_op jit(solution)/shard_map/qwji,qjk->qwik/dot_general | solution.py:38
  30.9 1.1 convolution_bitcast_fusion.24
  32.0 1.3 %collective-permute-start.5 = (f32[2,1,128,128]{3,2,1,0:T(8,128)S(1)}, f32[2,1,128,128]{3,2,1,0:T(8,128)S(1)}, u32[]{:S(2)}, u32[]{:S(2)}) collective-permute-start(f32[2,1,128,128]{3,2,1,0:T(8,128)S(1)} %pad_maximum_fusion.2), channel_id=1, source_target_pairs={{1,0},{2,1},{3,2},{5,4},{6,5},{7,6},{9,8},{10,9},{11,10},{13,12},{... | collective-permute-start | bytes 393224 | tf_op jit(solution)/shard_map/ppermute | solution.py:21
  33.3 4.7 %collective-permute-start.4 = (f32[2,1,128,128]{3,2,1,0:T(8,128)S(1)}, f32[2,1,128,128]{3,2,1,0:T(8,128)S(1)}, u32[]{:S(2)}, u32[]{:S(2)}) collective-permute-start(f32[2,1,128,128]{3,2,1,0:T(8,128)S(1)} %pad_maximum_fusion.2), channel_id=1, source_target_pairs={{0,1},{1,2},{2,3},{4,5},{5,6},{6,7},{8,9},{9,10},{10,11},{12,13},{... | collective-permute-start | bytes 393224 | tf_op jit(solution)/shard_map/ppermute | solution.py:18
  38.0 0.3 convolution_bitcast_fusion.17
  38.3 1.7 %collective-permute-done.4 = f32[2,1,128,128]{3,2,1,0:T(8,128)S(1)} collective-permute-done((f32[2,1,128,128]{3,2,1,0:T(8,128)S(1)}, f32[2,1,128,128]{3,2,1,0:T(8,128)S(1)}, u32[]{:S(2)}, u32[]{:S(2)}) %collective-permute-start.4) | collective-permute-done | bytes 131104 | tf_op jit(solution)/shard_map/ppermute | solution.py:18
  40.0 1.0 convolution_bitcast_fusion.6
  40.9 1.0 convolution_bitcast_fusion.23
  41.9 0.0 collective-permute-done.5
  42.0 0.3 fusion.35
  42.2 1.8 %convolution_bitcast_fusion.5 = f32[16,128,128]{2,1,0:T(8,128)S(1)} fusion(f32[1,1,16,128,128]{4,3,2,1,0:T(8,128)S(1)} %copy-done, f32[128,128]{1,0:T(8,128)S(1)} %fusion.35), kind=kOutput, calls=%fused_computation.5 | convolution fusion | flops 402653184 | bytes 2162688 | tf_op jit(solution)/shard_map/qwji,qjk->qwik/dot_general | solution.py:38
  44.1 1.1 convolution_bitcast_fusion.21
  45.2 1.3 %collective-permute-start.7 = (f32[2,1,128,128]{3,2,1,0:T(8,128)S(1)}, f32[2,1,128,128]{3,2,1,0:T(8,128)S(1)}, u32[]{:S(2)}, u32[]{:S(2)}) collective-permute-start(f32[2,1,128,128]{3,2,1,0:T(8,128)S(1)} %pad_maximum_fusion.3), channel_id=1, source_target_pairs={{1,0},{2,1},{3,2},{5,4},{6,5},{7,6},{9,8},{10,9},{11,10},{13,12},{... | collective-permute-start | bytes 393224 | tf_op jit(solution)/shard_map/ppermute | solution.py:21
  46.5 4.9 %collective-permute-start.6 = (f32[2,1,128,128]{3,2,1,0:T(8,128)S(1)}, f32[2,1,128,128]{3,2,1,0:T(8,128)S(1)}, u32[]{:S(2)}, u32[]{:S(2)}) collective-permute-start(f32[2,1,128,128]{3,2,1,0:T(8,128)S(1)} %pad_maximum_fusion.3), channel_id=1, source_target_pairs={{0,1},{1,2},{2,3},{4,5},{5,6},{6,7},{8,9},{9,10},{10,11},{12,13},{... | collective-permute-start | bytes 393224 | tf_op jit(solution)/shard_map/ppermute | solution.py:18
  51.5 0.3 convolution_bitcast_fusion.16
  51.7 1.4 %collective-permute-done.6 = f32[2,1,128,128]{3,2,1,0:T(8,128)S(1)} collective-permute-done((f32[2,1,128,128]{3,2,1,0:T(8,128)S(1)}, f32[2,1,128,128]{3,2,1,0:T(8,128)S(1)}, u32[]{:S(2)}, u32[]{:S(2)}) %collective-permute-start.6) | collective-permute-done | bytes 131104 | tf_op jit(solution)/shard_map/ppermute | solution.py:18
  53.2 1.0 convolution_bitcast_fusion.4
  54.1 1.0 convolution_bitcast_fusion.20
  55.1 0.0 collective-permute-done.7
  55.1 0.9 multiply_reduce_fusion
  56.0 11.5 %all-reduce = (f32[]{:T(128)}, f32[]{:T(128)}, f32[]{:T(128)}, f32[]{:T(128)}) all-reduce(f32[]{:T(128)S(6)} %convert_element_type.26, f32[]{:T(128)} %get-tuple-element.16, f32[]{:T(128)} %get-tuple-element.9, f32[]{:T(128)} %get-tuple-element.8), channel_id=1, replica_groups=mesh['seg'=8,'blk'=4] {'blk'}, use_global_device_ids=true, to_apply=%region_0.0 | all-reduce | flops 4 | bytes 32 | tf_op jit(solution)/shard_map/psum | solution.py:78
  68.9 0.3 convolution_bitcast_fusion.13
  69.2 0.3 convolution_bitcast_fusion.15
  69.5 1.0 convolution_bitcast_fusion.1
  70.5 1.1 convolution_bitcast_fusion.3
  71.6 0.3 convolution_bitcast_fusion.12
  71.9 0.3 convolution_bitcast_fusion.14
  72.2 1.1 convolution_bitcast_fusion
  73.3 1.0 convolution_bitcast_fusion.2
  74.2 0.1 maximum_multiply_fusion
  74.4 10.2 %collective-permute-start.8 = (f32[1,18,128,128]{2,3,1,0:T(8,128)S(1)}, f32[1,18,128,128]{2,3,1,0:T(8,128)}, u32[]{:S(2)}, u32[]{:S(2)}) collective-permute-start(f32[1,18,128,128]{2,3,1,0:T(8,128)S(1)} %maximum_multiply_fusion), channel_id=1, source_target_pairs={{0,4},{4,8},{8,12},{12,16},{16,20},{20,24},{24,28},{1,5},{5,9},{9,... | collective-permute-start | bytes 3538952 | tf_op jit(solution)/shard_map/ppermute | solution.py:29
  84.5 1.1 maximum_multiply_fusion.1
  85.7 1.9 %collective-permute-start.9 = (f32[1,18,128,128]{2,3,1,0:T(8,128)}, f32[1,18,128,128]{2,3,1,0:T(8,128)}, u32[]{:S(2)}, u32[]{:S(2)}) collective-permute-start(f32[1,18,128,128]{2,3,1,0:T(8,128)} %maximum_multiply_fusion.1), channel_id=1, source_target_pairs={{4,0},{8,4},{12,8},{16,12},{20,16},{24,20},{28,24},{5,1},{9,5},{13... | collective-permute-start | bytes 3538952 | tf_op jit(solution)/shard_map/ppermute | solution.py:29
  88.9 0.6 multiply_bitcast_fusion
  89.6 8.1 %collective-permute-done.8 = f32[1,18,128,128]{2,3,1,0:T(8,128)} collective-permute-done((f32[1,18,128,128]{2,3,1,0:T(8,128)S(1)}, f32[1,18,128,128]{2,3,1,0:T(8,128)}, u32[]{:S(2)}, u32[]{:S(2)}) %collective-permute-start.8) | collective-permute-done | bytes 1179680 | tf_op jit(solution)/shard_map/ppermute | solution.py:29
  97.7 2.7 %copy.13 = f32[1,1,18,128,128]{4,3,2,1,0:T(8,128)} copy(f32[1,1,18,128,128]{3,4,2,1,0:T(8,128)} %bitcast.68) | data formatting | bytes 2359296
  100.3 11.7 %collective-permute-done.9 = f32[1,18,128,128]{2,3,1,0:T(8,128)} collective-permute-done((f32[1,18,128,128]{2,3,1,0:T(8,128)}, f32[1,18,128,128]{2,3,1,0:T(8,128)}, u32[]{:S(2)}, u32[]{:S(2)}) %collective-permute-start.9) | collective-permute-done | bytes 1179680 | tf_op jit(solution)/shard_map/ppermute | solution.py:29
  112.1 2.7 %copy.14 = f32[1,1,18,128,128]{4,3,2,1,0:T(8,128)} copy(f32[1,1,18,128,128]{3,4,2,1,0:T(8,128)} %bitcast.79) | data formatting | bytes 2359296
  (11 shorter events, 0.1 us)
Async XLA Ops:
  0.6 1.8 %copy-start = (f32[1,1,16,128,128]{4,3,2,1,0:T(8,128)S(1)}, f32[1,1,16,128,128]{4,3,2,1,0:T(8,128)}, u32[]{:S(2)}) copy-start(f32[1,1,16,128,128]{4,3,2,1,0:T(8,128)} %param.10) | copy-start | bytes 3145732
  0.6 3.6 %copy-start.1 = (f32[1,1,16,128,128]{4,3,2,1,0:T(8,128)S(1)}, f32[1,1,16,128,128]{4,3,2,1,0:T(8,128)}, u32[]{:S(2)}) copy-start(f32[1,1,16,128,128]{4,3,2,1,0:T(8,128)} %param.11) | copy-start | bytes 3145732
  4.2 7.2 %copy-start.2 = (f32[1,1,2,128,128]{4,3,2,1,0:T(8,128)S(1)}, f32[1,1,2,128,128]{4,3,2,1,0:T(8,128)}, u32[]{:S(2)}) copy-start(f32[1,1,2,128,128]{4,3,2,1,0:T(8,128)} %param.8) | copy-start | bytes 393220
  5.4 10.1 %collective-permute-start.1 = (f32[2,1,128,128]{3,2,1,0:T(8,128)S(1)}, f32[2,1,128,128]{3,2,1,0:T(8,128)S(1)}, u32[]{:S(2)}, u32[]{:S(2)}) collective-permute-start(f32[2,1,128,128]{3,2,1,0:T(8,128)S(1)} %pad_maximum_fusion), channel_id=1, source_target_pairs={{1,0},{2,1},{3,2},{5,4},{6,5},{7,6},{9,8},{10,9},{11,10},{13,12},{... | collective-permute-start | bytes 393224 | tf_op jit(solution)/shard_map/ppermute | solution.py:21
  6.7 6.8 %collective-permute-start = (f32[2,1,128,128]{3,2,1,0:T(8,128)S(1)}, f32[2,1,128,128]{3,2,1,0:T(8,128)S(1)}, u32[]{:S(2)}, u32[]{:S(2)}) collective-permute-start(f32[2,1,128,128]{3,2,1,0:T(8,128)S(1)} %pad_maximum_fusion), channel_id=1, source_target_pairs={{0,1},{1,2},{2,3},{4,5},{5,6},{6,7},{8,9},{9,10},{10,11},{12,13},{... | collective-permute-start | bytes 393224 | tf_op jit(solution)/shard_map/ppermute | solution.py:18
  14.5 1.0 copy-start.3
  14.5 1.0 copy-start.4
  18.8 10.0 %collective-permute-start.3 = (f32[2,1,128,128]{3,2,1,0:T(8,128)S(1)}, f32[2,1,128,128]{3,2,1,0:T(8,128)S(1)}, u32[]{:S(2)}, u32[]{:S(2)}) collective-permute-start(f32[2,1,128,128]{3,2,1,0:T(8,128)S(1)} %pad_maximum_fusion.1), channel_id=1, source_target_pairs={{1,0},{2,1},{3,2},{5,4},{6,5},{7,6},{9,8},{10,9},{11,10},{13,12},{... | collective-permute-start | bytes 393224 | tf_op jit(solution)/shard_map/ppermute | solution.py:21
  20.1 6.7 %collective-permute-start.2 = (f32[2,1,128,128]{3,2,1,0:T(8,128)S(1)}, f32[2,1,128,128]{3,2,1,0:T(8,128)S(1)}, u32[]{:S(2)}, u32[]{:S(2)}) collective-permute-start(f32[2,1,128,128]{3,2,1,0:T(8,128)S(1)} %pad_maximum_fusion.1), channel_id=1, source_target_pairs={{0,1},{1,2},{2,3},{4,5},{5,6},{6,7},{8,9},{9,10},{10,11},{12,13},{... | collective-permute-start | bytes 393224 | tf_op jit(solution)/shard_map/ppermute | solution.py:18
  32.0 9.9 %collective-permute-start.5 = (f32[2,1,128,128]{3,2,1,0:T(8,128)S(1)}, f32[2,1,128,128]{3,2,1,0:T(8,128)S(1)}, u32[]{:S(2)}, u32[]{:S(2)}) collective-permute-start(f32[2,1,128,128]{3,2,1,0:T(8,128)S(1)} %pad_maximum_fusion.2), channel_id=1, source_target_pairs={{1,0},{2,1},{3,2},{5,4},{6,5},{7,6},{9,8},{10,9},{11,10},{13,12},{... | collective-permute-start | bytes 393224 | tf_op jit(solution)/shard_map/ppermute | solution.py:21
  33.3 6.6 %collective-permute-start.4 = (f32[2,1,128,128]{3,2,1,0:T(8,128)S(1)}, f32[2,1,128,128]{3,2,1,0:T(8,128)S(1)}, u32[]{:S(2)}, u32[]{:S(2)}) collective-permute-start(f32[2,1,128,128]{3,2,1,0:T(8,128)S(1)} %pad_maximum_fusion.2), channel_id=1, source_target_pairs={{0,1},{1,2},{2,3},{4,5},{5,6},{6,7},{8,9},{9,10},{10,11},{12,13},{... | collective-permute-start | bytes 393224 | tf_op jit(solution)/shard_map/ppermute | solution.py:18
  45.2 9.9 %collective-permute-start.7 = (f32[2,1,128,128]{3,2,1,0:T(8,128)S(1)}, f32[2,1,128,128]{3,2,1,0:T(8,128)S(1)}, u32[]{:S(2)}, u32[]{:S(2)}) collective-permute-start(f32[2,1,128,128]{3,2,1,0:T(8,128)S(1)} %pad_maximum_fusion.3), channel_id=1, source_target_pairs={{1,0},{2,1},{3,2},{5,4},{6,5},{7,6},{9,8},{10,9},{11,10},{13,12},{... | collective-permute-start | bytes 393224 | tf_op jit(solution)/shard_map/ppermute | solution.py:21
  46.5 6.6 %collective-permute-start.6 = (f32[2,1,128,128]{3,2,1,0:T(8,128)S(1)}, f32[2,1,128,128]{3,2,1,0:T(8,128)S(1)}, u32[]{:S(2)}, u32[]{:S(2)}) collective-permute-start(f32[2,1,128,128]{3,2,1,0:T(8,128)S(1)} %pad_maximum_fusion.3), channel_id=1, source_target_pairs={{0,1},{1,2},{2,3},{4,5},{5,6},{6,7},{8,9},{9,10},{10,11},{12,13},{... | collective-permute-start | bytes 393224 | tf_op jit(solution)/shard_map/ppermute | solution.py:18
  74.4 23.3 %collective-permute-start.8 = (f32[1,18,128,128]{2,3,1,0:T(8,128)S(1)}, f32[1,18,128,128]{2,3,1,0:T(8,128)}, u32[]{:S(2)}, u32[]{:S(2)}) collective-permute-start(f32[1,18,128,128]{2,3,1,0:T(8,128)S(1)} %maximum_multiply_fusion), channel_id=1, source_target_pairs={{0,4},{4,8},{8,12},{12,16},{16,20},{20,24},{24,28},{1,5},{5,9},{9,... | collective-permute-start | bytes 3538952 | tf_op jit(solution)/shard_map/ppermute | solution.py:29
  85.7 26.4 %collective-permute-start.9 = (f32[1,18,128,128]{2,3,1,0:T(8,128)}, f32[1,18,128,128]{2,3,1,0:T(8,128)}, u32[]{:S(2)}, u32[]{:S(2)}) collective-permute-start(f32[1,18,128,128]{2,3,1,0:T(8,128)} %maximum_multiply_fusion.1), channel_id=1, source_target_pairs={{4,0},{8,4},{12,8},{16,12},{20,16},{24,20},{28,24},{5,1},{9,5},{13... | collective-permute-start | bytes 3538952 | tf_op jit(solution)/shard_map/ppermute | solution.py:29
where the time goes:
time: 116 us
  starting transfers between devices  36.5 us (31%)
  matrix products  27.7 us (24%)
  waiting for transfers between devices  25.6 us (22%)
  blocking collectives  11.5 us (10%)
  between operations  6.41 us (6%)
  local copies, waits for them, and re-layouts  5.34 us (5%)
  other arithmetic  2.86 us (2%)
    ppermute x2, waiting for transfers between devices, passed_along(): lax.ppermute(value, axis, [(source, source + steps) for source in range(l...  19.8 us
    ppermute x4, starting transfers between devices, padded_2(): lax.ppermute(lax.slice_in_dim(block, block.shape[dim] - width, None, axis...  19.2 us
    ppermute x2, starting transfers between devices, passed_along(): lax.ppermute(value, axis, [(source, source + steps) for source in range(l...  12.1 us
    psum x1, blocking collectives, shards(): lax.psum((jnp.sum(last_vector * last_applied), jnp.sum(last_vector * last...  11.5 us
    dot_general x4, matrix products, channel_adjoint(): halfway = jnp.einsum('qwji,qjk->qwik', left_ops, vector, precision=highest)  7.22 us
    ppermute x4, waiting for transfers between devices, padded_2(): lax.ppermute(lax.slice_in_dim(block, block.shape[dim] - width, None, axis...  5.77 us
    dot_general x8, matrix products, channel_apply(): return jnp.einsum('qwik,qwlk->qil', halfway, right_ops, precision=highest)  5.72 us
    unnamed x12, local copies, waits for them, and re-layouts  5.34 us
  transfers between devices with their start and end apart: 10, of which 6 were waited for; matrix products, arithmetic and copies ran while one was open for 11% of the time, Pallas kernels for 0%

commit v1 on v0

v1 whole, which is shorter than its diff:
```python
import functools

import jax
import jax.numpy as jnp
from jax import lax
from jax.experimental import pallas as pl
from jax.experimental.pallas import tpu as pltpu
from jax.sharding import PartitionSpec as P

ITERS = 4
MESH = pl.DeviceIdType.MESH
f32 = jnp.float32
bf16 = jnp.bfloat16
spectral_shift = 20.0


def split(x):
    hi = x.astype(bf16)
    lo = (x - hi.astype(f32)).astype(bf16)
    return hi, lo


def stationary(x):
    hi, lo = split(x)
    top = jnp.concatenate([hi, lo], 1)
    low = jnp.concatenate([hi, jnp.zeros_like(hi)], 1)
    return jnp.concatenate([top, low], 0)


def streamed(x):
    hi, lo = split(x)
    top = jnp.concatenate([hi, hi], 1)
    low = jnp.concatenate([lo, jnp.zeros_like(lo)], 1)
    return jnp.concatenate([top, low], 0)


def dot(a, b):
    return jnp.dot(a, b, preferred_element_type=f32)


def prepare(source, rows, target, at, transpose, n):
    x = source[pl.ds(rows, n), :]
    hi, lo = split(x.T if transpose else x)
    target[pl.ds(at, n), 0:n] = hi
    target[pl.ds(at, n), n : 2 * n] = lo


def first_stage(ops, start, count, weight, held, column, n):
    for c in range(0, count, 2):
        got = dot(ops[start + c * n : start + (c + 2) * n, :], weight)
        got = got[:, 0:n] + got[:, n : 2 * n]
        hi, lo = split(got)
        for part in range(2):
            lanes = column + (c + part) * n
            held[0:n, lanes : lanes + n] = hi[part * n : (part + 1) * n]
            held[n : 2 * n, lanes : lanes + n] = lo[part * n : (part + 1) * n]


def second_stage(held, column, count, ops, start, n):
    got = dot(held[:, column : column + count * n], ops[start : start + count * n, :])
    return (got[0:n, 0:n] + got[0:n, n : 2 * n]) + (got[n : 2 * n, 0:n] + got[n : 2 * n, n : 2 * n])


def extend(ops, state, state_t, out, scale, count, n):
    weight = stationary(state)
    rows = streamed(state_t)
    for c in range(0, count, 2):
        got = dot(ops[c * n : (c + 2) * n, :], weight)
        got = got[:, 0:n] + got[:, n : 2 * n]
        hi, lo = split(got)
        pair = jnp.concatenate(
            [jnp.concatenate([hi[0:n], hi[n:]], 1), jnp.concatenate([lo[0:n], lo[n:]], 1)], 0
        )
        done = dot(rows, pair)
        done = (done[0:n] + done[n:]) * scale
        out[c * n : (c + 1) * n, :] = done[:, 0:n]
        out[(c + 1) * n : (c + 2) * n, :] = done[:, n : 2 * n]


def kernel(
    nseg, nblk, ndiag, nhop, n,
    size_ref, rank_ref, two_ref, dl_ref, dr_ref, hl_ref, hr_ref,
    state_ref, lb_ref, rb_ref, energy_ref,
    xl, yr, far_x, far_y, a2, at2, b2, bt2, fx2, fy2, held,
    v_buf, c_buf, rv, rc, kept, far_kept, sums,
    load_sem, v_send, v_recv, c_send, c_recv, x_send, x_recv, k_send, k_recv, s_send, s_recv,
):
    s = lax.axis_index("seg")
    q = lax.axis_index("blk")
    nch = ndiag + nhop
    small = ndiag * n

    loads = [
        pltpu.make_async_copy(src, dst, load_sem.at[i])
        for i, (src, dst) in enumerate(
            (
                (two_ref, c_buf.at[ITERS]),
                (hl_ref, xl.at[pl.ds(small, nhop * n)]),
                (hr_ref, yr.at[pl.ds(small, nhop * n)]),
                (dl_ref, xl.at[pl.ds(0, small)]),
                (dr_ref, yr.at[pl.ds(0, small)]),
            )
        )
    ]
    for load in loads:
        load.start()

    def per_segment(action):
        action(0)
        pl.when(s < nseg - 1)(lambda: action(1))
        pl.when(s > 0)(lambda: action(-1))

    def per_peer(step, action):
        def body(j, carry):
            action(lax.rem(q + j, nblk), j)
            return carry

        lax.fori_loop(1 if step == 0 else 0, nblk, body, 0, unroll=nblk <= 8)

    barrier = pltpu.get_barrier_semaphore()

    def greet(step):
        per_peer(
            step,
            lambda peer, j: pl.semaphore_signal(
                barrier, inc=1, device_id={"seg": s + step, "blk": peer}, device_id_type=MESH
            ),
        )

    per_segment(greet)

    @pl.when(q == 0)
    def _():
        rv[...] = jnp.zeros_like(rv)

    @pl.when(q == nblk - 1)
    def _():
        rc[...] = jnp.zeros_like(rc)

    size = size_ref[0, 0]
    count = jnp.minimum(rank_ref[0, 0], size)
    row_at = lax.broadcasted_iota(jnp.int32, (n, n), 0)
    col_at = lax.broadcasted_iota(jnp.int32, (n, n), 1)
    live = jnp.where(jnp.maximum(row_at, col_at) < size, 1.0, 0.0).astype(f32)
    col_live = jnp.where(col_at < count, 1.0, 0.0).astype(f32)

    loads[0].wait()
    v_buf[0] = live * c_buf[ITERS]

    groups = 1 + jnp.minimum(s, 1) + jnp.minimum(nseg - 1 - s, 1)
    pl.semaphore_wait(barrier, groups * nblk - 1)

    def remote(src, dst, send, recv, where):
        return pltpu.make_async_remote_copy(
            src_ref=src, dst_ref=dst, send_sem=send, recv_sem=recv,
            device_id=where, device_id_type=MESH,
        )

    def send_v(k):
        return remote(v_buf.at[k], rv.at[k], v_send.at[k], v_recv.at[k], {"seg": s, "blk": q + 1})

    def send_c(k):
        return remote(c_buf.at[k], rc.at[k], c_send.at[k], c_recv.at[k], {"seg": s, "blk": q - 1})

    up, down = {"seg": s + 1, "blk": q}, {"seg": s - 1, "blk": q}
    to_up = [
        remote(dl_ref, far_x.at[pl.ds(0, small)], x_send.at[0], x_recv.at[0], up),
        remote(hl_ref, far_x.at[pl.ds(small, nhop * n)], x_send.at[1], x_recv.at[1], up),
    ]
    to_down = [
        remote(dr_ref, far_y.at[pl.ds(0, small)], x_send.at[2], x_recv.at[2], down),
        remote(hr_ref, far_y.at[pl.ds(small, nhop * n)], x_send.at[3], x_recv.at[3], down),
    ]
    kept_up = remote(kept, far_kept.at[0], k_send.at[0], k_recv.at[0], up)
    kept_down = remote(kept, far_kept.at[1], k_send.at[1], k_recv.at[1], down)

    has_next, has_previous = q < nblk - 1, q > 0
    has_up, has_down = s < nseg - 1, s > 0

    pl.when(has_next)(lambda: send_v(0).start())

    @pl.when(has_up)
    def _():
        for copy in to_up:
            copy.start()

    @pl.when(has_down)
    def _():
        for copy in to_down:
            copy.start()

    loads[1].wait()
    loads[2].wait()
    for h in range(nhop):
        at = small + h * n
        prepare(xl, at, at2, h * n, True, n)
        prepare(yr, at, b2, h * n, False, n)

    def carried(k):
        first_stage(at2, 0, nhop, stationary(v_buf[k]), held, 0, n)
        c_buf[k] = second_stage(held, 0, nhop, b2, 0, n)
        pl.when(has_previous)(lambda: send_c(k).start())

    def finish(k):
        first_stage(a2, 0, ndiag, stationary(v_buf[k]), held, 0, n)
        pl.when(has_previous)(lambda: send_v(k).wait_recv())
        first_stage(a2, small, nhop, stationary(rv[k]), held, small, n)
        own = second_stage(held, 0, nch, bt2, 0, n)
        pl.when(has_next)(lambda: send_c(k).wait_recv())
        applied = live * (own + rc[k])
        vector = spectral_shift * v_buf[k] - applied
        v_buf[k + 1] = vector
        return applied, vector

    carried(0)
    loads[3].wait()
    loads[4].wait()
    for c in range(nch):
        prepare(xl, c * n, a2, c * n, False, n)
        prepare(yr, c * n, bt2, c * n, True, n)
    finish(0)
    pl.when(has_next)(lambda: send_v(1).start())

    def middle(k, carry):
        carried(k)
        finish(k)
        pl.when(has_next)(lambda: send_v(k + 1).start())
        return carry

    lax.fori_loop(1, ITERS - 1, middle, 0)
    carried(ITERS - 1)
    applied, vector = finish(ITERS - 1)
    last = v_buf[ITERS - 1]
    kept[...] = vector * col_live
    pl.when(has_up)(lambda: kept_up.start())
    pl.when(has_down)(lambda: kept_down.start())

    def rowsum(x):
        return jnp.sum(x, 0, keepdims=True)

    row8 = lax.broadcasted_iota(jnp.int32, (8, n), 0)
    tile = jnp.where(row8 == 0, rowsum(last * applied), 0.0)
    tile = jnp.where(row8 == 1, rowsum(last * last), tile)
    tile = jnp.where(row8 == 2, rowsum(vector * vector), tile)
    tile = jnp.where(row8 == 3, size.astype(f32) * (1.0 / n), tile)
    sums[1, q] = tile

    def sum_copy(step, peer, j):
        group = 1 - step
        return remote(
            sums.at[1, q], sums.at[group, q], s_send.at[group, j], s_recv.at[group, q],
            {"seg": s + step, "blk": peer},
        )

    def sum_arrival(group, peer):
        return remote(
            sums.at[1, q], sums.at[group, peer], s_send.at[group, 0], s_recv.at[group, peer],
            {"seg": s, "blk": peer},
        )

    per_segment(lambda step: per_peer(step, lambda peer, j: sum_copy(step, peer, j).start()))

    @pl.when(has_down)
    def _():
        for copy in to_up:
            copy.wait_recv()
        for c in range(nch):
            prepare(far_x, c * n, fx2, c * n, False, n)

    @pl.when(has_up)
    def _():
        for copy in to_down:
            copy.wait_recv()
        for c in range(nch):
            prepare(far_y, c * n, fy2, c * n, True, n)

    def totals(group):
        step = 0 if group == 1 else 1
        per_peer(step, lambda peer, j: sum_arrival(group, peer).wait_recv())
        total = sums[group, 0]
        for j in range(1, nblk):
            total = total + sums[group, j]
        return jnp.sum(total, 1, keepdims=True)

    def norm(total):
        return jnp.sqrt(total[3:4] * n / total[2:3])

    own = totals(1)
    state_ref[...] = vector * norm(own)
    energy_ref[...] = own[0:1] / own[1:2]
    scale = 1.0 / jnp.sqrt(f32(n))

    @pl.when(has_down)
    def _():
        kept_up.wait_recv()
        k = far_kept[0] * norm(totals(0))
        extend(fx2, k, k.T, lb_ref, scale, nch, n)

    @pl.when(s == 0)
    def _():
        lb_ref[...] = jnp.zeros_like(lb_ref)

    @pl.when(has_up)
    def _():
        kept_down.wait_recv()
        k = far_kept[1] * norm(totals(2))
        extend(fy2, k.T, k, rb_ref, scale, nch, n)

    @pl.when(s == nseg - 1)
    def _():
        rb_ref[...] = jnp.zeros_like(rb_ref)

    @pl.when(has_next)
    def _():
        for k in range(ITERS):
            send_v(k).wait_send()

    @pl.when(has_previous)
    def _():
        for k in range(ITERS):
            send_c(k).wait_send()

    @pl.when(has_up)
    def _():
        for copy in to_up + [kept_up]:
            copy.wait_send()

    @pl.when(has_down)
    def _():
        for copy in to_down + [kept_down]:
            copy.wait_send()

    per_segment(lambda step: per_peer(step, lambda peer, j: sum_copy(step, peer, j).wait_send()))


def shards(nseg, nblk, two_site, diag_left, diag_right, hop_left, hop_right, sector_sizes, ranks):
    n = two_site.shape[2]
    ndiag, nhop = diag_left.shape[2], hop_left.shape[2]
    nch = ndiag + nhop
    smem = pl.BlockSpec(memory_space=pltpu.SMEM)
    vmem = pl.BlockSpec(memory_space=pltpu.VMEM)
    anywhere = pl.BlockSpec(memory_space=pl.ANY)
    dma = pltpu.SemaphoreType.DMA
    state, left, right, energy = pl.pallas_call(
        functools.partial(kernel, nseg, nblk, ndiag, nhop, n),
        out_shape=(
            jax.ShapeDtypeStruct((n, n), f32),
            jax.ShapeDtypeStruct((nch * n, n), f32),
            jax.ShapeDtypeStruct((nch * n, n), f32),
            jax.ShapeDtypeStruct((1, 1), f32),
        ),
        in_specs=[smem, smem] + [anywhere] * 5,
        out_specs=(vmem, vmem, vmem, vmem),
        scratch_shapes=[
            pltpu.VMEM((nch * n, n), f32),
            pltpu.VMEM((nch * n, n), f32),
            pltpu.VMEM((nch * n, n), f32),
            pltpu.VMEM((nch * n, n), f32),
            pltpu.VMEM((nch * n, 2 * n), bf16),
            pltpu.VMEM((nhop * n, 2 * n), bf16),
            pltpu.VMEM((nhop * n, 2 * n), bf16),
            pltpu.VMEM((nch * n, 2 * n), bf16),
            pltpu.VMEM((nch * n, 2 * n), bf16),
            pltpu.VMEM((nch * n, 2 * n), bf16),
            pltpu.VMEM((2 * n, nch * n), bf16),
            pltpu.VMEM((ITERS + 1, n, n), f32),
            pltpu.VMEM((ITERS + 1, n, n), f32),
            pltpu.VMEM((ITERS, n, n), f32),
            pltpu.VMEM((ITERS, n, n), f32),
            pltpu.VMEM((n, n), f32),
            pltpu.VMEM((2, n, n), f32),
            pltpu.VMEM((3, nblk, 8, n), f32),
            dma((5,)),
            dma((ITERS,)),
            dma((ITERS,)),
            dma((ITERS,)),
            dma((ITERS,)),
            dma((4,)),
            dma((4,)),
            dma((2,)),
            dma((2,)),
            dma((3, nblk)),
            dma((3, nblk)),
        ],
        compiler_params=pltpu.CompilerParams(
            collective_id=0, has_side_effects=True, vmem_limit_bytes=40 * 1024 * 1024
        ),
        name="solve",
    )(
        sector_sizes, ranks,
        two_site.reshape(n, n),
        diag_left.reshape(ndiag * n, n),
        diag_right.reshape(ndiag * n, n),
        hop_left.reshape(nhop * n, n),
        hop_right.reshape(nhop * n, n),
    )
    return (
        state.reshape(1, 1, n, n),
        left.reshape(1, 1, nch, n, n),
        right.reshape(1, 1, nch, n, n),
        energy.reshape(1),
    )


def solution(mesh):
    nseg, nblk = mesh.shape["seg"], mesh.shape["blk"]
    return jax.shard_map(
        functools.partial(shards, nseg, nblk),
        mesh=mesh,
        in_specs=(
            P("seg", "blk", None, None),
            P("seg", "blk", None, None, None),
            P("seg", "blk", None, None, None),
            P("seg", "blk", None, None, None),
            P("seg", "blk", None, None, None),
            P("seg", "blk"),
            P("seg", "blk"),
        ),
        out_specs=(
            P("seg", "blk", None, None),
            P("seg", "blk", None, None, None),
            P("seg", "blk", None, None, None),
            P("seg"),
        ),
        check_vma=False,
    )
```

time: 116 us -> 49.2 us (0.42)
  Pallas kernels: 0 us -> 37.1 us
  starting transfers between devices: 36.5 us -> 0 us
  matrix products: 27.7 us -> 0 us
  waiting for transfers between devices: 25.6 us -> 0 us
  blocking collectives: 11.5 us -> 0 us
  other arithmetic: 2.86 us -> 0 us
  between operations: 6.41 us -> 3.64 us
  local copies, waits for them, and re-layouts: 5.34 us -> 7.75 us
    pallas_call x0 -> x1, Pallas kernels: none -> 37.1 us  [shards(): pl.pallas_call(functools.partial(kernel, nseg, nblk, ndiag, nhop, n), out...]
    ppermute x10 -> x0, starting transfers between devices: 36.5 us -> none  [the longest x4 19.2 us: padded_2(): lax.ppermute(lax.slice_in_dim(block, block.shape[dim] - width, None, axis...]
    dot_general x32 -> x0, matrix products: 27.7 us -> none  [the longest x4 7.22 us: channel_adjoint(): halfway = jnp.einsum('qwji,qjk->qwik', left_ops, vector, precision=highest)]
    ppermute x10 -> x0, waiting for transfers between devices: 25.6 us -> none  [the longest x2 19.8 us: passed_along(): lax.ppermute(value, axis, [(source, source + steps) for source in range(l...]
    psum x1 -> x0, blocking collectives: 11.5 us -> none  [shards(): lax.psum((jnp.sum(last_vector * last_applied), jnp.sum(last_vector * last...]
    unnamed x12 -> x13, local copies, waits for them, and re-layouts: 5.34 us -> 7.75 us
    mul x3 -> x0, other arithmetic: 2.17 us -> none  [the longest x1 1.12 us: shards(): jnp.concatenate([right_extend(kept_state, keep_right), right_extend(kept_...]
  transfers between devices with their start and end apart: 10 -> 0, of which waited for: 6 -> 0; matrix products, arithmetic and copies ran while one was open for 11% -> 0% of each run, Pallas kernels for 0% -> 0%
where the time goes in v1:
time: 49.2 us; the launch traced here: 48.4 us
  Pallas kernels  37.1 us (75%)
  local copies, waits for them, and re-layouts  7.75 us (16%)
  between operations  3.64 us (7%)
    pallas_call x1, Pallas kernels, shards(): pl.pallas_call(functools.partial(kernel, nseg, nblk, ndiag, nhop, n), out...  37.1 us
    unnamed x13, local copies, waits for them, and re-layouts  7.75 us

profile of v1, /device:TPU:1, one launch (start us, length us, event | category | flops | bytes accessed | tf_op | source)
XLA Modules:
  0.0 48.4 jit_solution(11866934061623506962)
XLA Ops:
  1.9 0.0 copy-start
  1.9 1.2 %copy-done = f32[1,1,16,128,128]{4,3,2,1,0:T(8,128)S(1)} copy-done((f32[1,1,16,128,128]{4,3,2,1,0:T(8,128)S(1)}, f32[1,1,16,128,128]{4,3,2,1,0:T(8,128)}, u32[]{:S(2)}) %copy-start) | copy-done | bytes 1048600
  3.1 0.0 copy-start.1
  3.2 1.2 %copy-done.1 = f32[1,1,16,128,128]{4,3,2,1,0:T(8,128)S(1)} copy-done((f32[1,1,16,128,128]{4,3,2,1,0:T(8,128)S(1)}, f32[1,1,16,128,128]{4,3,2,1,0:T(8,128)}, u32[]{:S(2)}) %copy-start.1) | copy-done | bytes 1048600
  4.4 0.0 copy-start.2
  4.4 0.9 %copy-done.2 = f32[1,1,2,128,128]{4,3,2,1,0:T(8,128)S(1)} copy-done((f32[1,1,2,128,128]{4,3,2,1,0:T(8,128)S(1)}, f32[1,1,2,128,128]{4,3,2,1,0:T(8,128)}, u32[]{:S(2)}) %copy-start.2) | copy-done | bytes 131096
  5.3 0.0 copy-start.3
  5.3 0.9 %copy-done.3 = f32[1,1,2,128,128]{4,3,2,1,0:T(8,128)S(1)} copy-done((f32[1,1,2,128,128]{4,3,2,1,0:T(8,128)S(1)}, f32[1,1,2,128,128]{4,3,2,1,0:T(8,128)}, u32[]{:S(2)}) %copy-start.3) | copy-done | bytes 131096
  6.2 0.0 copy-start.4
  6.2 0.8 %copy-done.4 = f32[1,1,128,128]{3,2,1,0:T(8,128)S(1)} copy-done((f32[1,1,128,128]{3,2,1,0:T(8,128)S(1)}, f32[1,1,128,128]{3,2,1,0:T(8,128)}, u32[]{:S(2)}) %copy-start.4) | copy-done | bytes 65560
  7.0 37.1 %solve.1 = (f32[128,128]{1,0:T(8,128)S(1)}, f32[2304,128]{1,0:T(8,128)S(1)}, f32[2304,128]{1,0:T(8,128)S(1)}, f32[1,1]{1,0:T(1,128)}) custom-call(s32[1,1]{1,0:T(1,128)S(6)} %copy.15.size_ref, s32[1,1]{1,0:T(1,128)S(6)} %copy.16.rank_ref, f32[128,128]{1,0:T(8,128)S(1)} %bitcast.15, f32[256,128]{1,0:T(8,128)S(1)} %bitcast.13, f32[256,128]{1,0:T(8,128)S(1)} %bitcast.14, ...), custom_call_target="tpu_custom_call" | custom-call | tf_op jit(solution)/shard_map/solve/pallas_call | solution.py:344
  44.1 0.6 %copy.17 = f32[1,1,128,128]{3,2,1,0:T(8,128)} copy(f32[1,1,128,128]{3,2,1,0:T(8,128)S(1)} %bitcast.16) | data formatting | bytes 131072
  44.7 1.0 %copy.18 = f32[1,1,18,128,128]{4,3,2,1,0:T(8,128)} copy(f32[1,1,18,128,128]{4,3,2,1,0:T(8,128)S(1)} %bitcast.10) | data formatting | bytes 2359296
  45.7 1.0 %copy.19 = f32[1,1,18,128,128]{4,3,2,1,0:T(8,128)} copy(f32[1,1,18,128,128]{4,3,2,1,0:T(8,128)S(1)} %bitcast.9) | data formatting | bytes 2359296
Async XLA Ops:
  1.9 1.2 %copy-start = (f32[1,1,16,128,128]{4,3,2,1,0:T(8,128)S(1)}, f32[1,1,16,128,128]{4,3,2,1,0:T(8,128)}, u32[]{:S(2)}) copy-start(f32[1,1,16,128,128]{4,3,2,1,0:T(8,128)} %param.10) | copy-start | bytes 3145732
  3.1 1.2 %copy-start.1 = (f32[1,1,16,128,128]{4,3,2,1,0:T(8,128)S(1)}, f32[1,1,16,128,128]{4,3,2,1,0:T(8,128)}, u32[]{:S(2)}) copy-start(f32[1,1,16,128,128]{4,3,2,1,0:T(8,128)} %param.11) | copy-start | bytes 3145732
  4.4 0.9 %copy-start.2 = (f32[1,1,2,128,128]{4,3,2,1,0:T(8,128)S(1)}, f32[1,1,2,128,128]{4,3,2,1,0:T(8,128)}, u32[]{:S(2)}) copy-start(f32[1,1,2,128,128]{4,3,2,1,0:T(8,128)} %param.8) | copy-start | bytes 393220
  5.3 0.9 %copy-start.3 = (f32[1,1,2,128,128]{4,3,2,1,0:T(8,128)S(1)}, f32[1,1,2,128,128]{4,3,2,1,0:T(8,128)}, u32[]{:S(2)}) copy-start(f32[1,1,2,128,128]{4,3,2,1,0:T(8,128)} %param.9) | copy-start | bytes 393220
  6.2 0.8 %copy-start.4 = (f32[1,1,128,128]{3,2,1,0:T(8,128)S(1)}, f32[1,1,128,128]{3,2,1,0:T(8,128)}, u32[]{:S(2)}) copy-start(f32[1,1,128,128]{3,2,1,0:T(8,128)} %param.7) | copy-start | bytes 196612

commit v2 on v1

--- a/solution.py
+++ b/solution.py
@@ -8,6 +8,7 @@
 from jax.sharding import PartitionSpec as P
 
 ITERS = 4
+BATCH = 8
 MESH = pl.DeviceIdType.MESH
 f32 = jnp.float32
 bf16 = jnp.bfloat16
@@ -46,11 +47,12 @@
 
 
 def first_stage(ops, start, count, weight, held, column, n):
-    for c in range(0, count, 2):
-        got = dot(ops[start + c * n : start + (c + 2) * n, :], weight)
+    for c in range(0, count, BATCH):
+        size = min(BATCH, count - c)
+        got = dot(ops[start + c * n : start + (c + size) * n, :], weight)
         got = got[:, 0:n] + got[:, n : 2 * n]
         hi, lo = split(got)
-        for part in range(2):
+        for part in range(size):
             lanes = column + (c + part) * n
             held[0:n, lanes : lanes + n] = hi[part * n : (part + 1) * n]
             held[n : 2 * n, lanes : lanes + n] = lo[part * n : (part + 1) * n]
@@ -61,29 +63,26 @@
     return (got[0:n, 0:n] + got[0:n, n : 2 * n]) + (got[n : 2 * n, 0:n] + got[n : 2 * n, n : 2 * n])
 
 
-def extend(ops, state, state_t, out, scale, count, n):
-    weight = stationary(state)
-    rows = streamed(state_t)
-    for c in range(0, count, 2):
-        got = dot(ops[c * n : (c + 2) * n, :], weight)
-        got = got[:, 0:n] + got[:, n : 2 * n]
-        hi, lo = split(got)
-        pair = jnp.concatenate(
-            [jnp.concatenate([hi[0:n], hi[n:]], 1), jnp.concatenate([lo[0:n], lo[n:]], 1)], 0
-        )
-        done = dot(rows, pair)
-        done = (done[0:n] + done[n:]) * scale
-        out[c * n : (c + 1) * n, :] = done[:, 0:n]
-        out[(c + 1) * n : (c + 2) * n, :] = done[:, n : 2 * n]
+def extend(ops, weight, rows, out, scale, start, count, n):
+    got = dot(ops[start : start + count * n, :], weight)
+    got = got[:, 0:n] + got[:, n : 2 * n]
+    hi, lo = split(got)
+    tops = [hi[c * n : (c + 1) * n] for c in range(count)]
+    lows = [lo[c * n : (c + 1) * n] for c in range(count)]
+    wide = jnp.concatenate([jnp.concatenate(tops, 1), jnp.concatenate(lows, 1)], 0)
+    done = dot(rows, wide)
+    done = (done[0:n] + done[n:]) * scale
+    for c in range(count):
+        out[start + c * n : start + (c + 1) * n, :] = done[:, c * n : (c + 1) * n]
 
 
 def kernel(
     nseg, nblk, ndiag, nhop, n,
     size_ref, rank_ref, two_ref, dl_ref, dr_ref, hl_ref, hr_ref,
     state_ref, lb_ref, rb_ref, energy_ref,
-    xl, yr, far_x, far_y, a2, at2, b2, bt2, fx2, fy2, held,
+    xl, yr, far_x, far_y, state_v, lb_v, rb_v, a2, at2, b2, bt2, fx2, fy2, held,
     v_buf, c_buf, rv, rc, kept, far_kept, sums,
-    load_sem, v_send, v_recv, c_send, c_recv, x_send, x_recv, k_send, k_recv, s_send, s_recv,
+    load_sem, v_send, v_recv, c_send, c_recv, x_send, x_recv, k_send, k_recv, s_send, s_recv, out_sem,
 ):
     s = lax.axis_index("seg")
     q = lax.axis_index("blk")
@@ -163,14 +162,21 @@
         return remote(c_buf.at[k], rc.at[k], c_send.at[k], c_recv.at[k], {"seg": s, "blk": q - 1})
 
     up, down = {"seg": s + 1, "blk": q}, {"seg": s - 1, "blk": q}
-    to_up = [
-        remote(dl_ref, far_x.at[pl.ds(0, small)], x_send.at[0], x_recv.at[0], up),
-        remote(hl_ref, far_x.at[pl.ds(small, nhop * n)], x_send.at[1], x_recv.at[1], up),
-    ]
-    to_down = [
-        remote(dr_ref, far_y.at[pl.ds(0, small)], x_send.at[2], x_recv.at[2], down),
-        remote(hr_ref, far_y.at[pl.ds(small, nhop * n)], x_send.at[3], x_recv.at[3], down),
-    ]
+    half = nhop // 2 * n
+    chunks = [(small, half, 1), (small + half, nhop * n - half, 1), (0, small, 0)]
+
+    def environment(refs, far, first, where):
+        return [
+            remote(
+                refs[hop].at[pl.ds(start - small * hop, rows)],
+                far.at[pl.ds(start, rows)],
+                x_send.at[first + i], x_recv.at[first + i], where,
+            )
+            for i, (start, rows, hop) in enumerate(chunks)
+        ]
+
+    to_up = environment((dl_ref, hl_ref), far_x, 0, up)
+    to_down = environment((dr_ref, hr_ref), far_y, 3, down)
     kept_up = remote(kept, far_kept.at[0], k_send.at[0], k_recv.at[0], up)
     kept_down = remote(kept, far_kept.at[1], k_send.at[1], k_recv.at[1], down)
 
@@ -260,20 +266,6 @@
 
     per_segment(lambda step: per_peer(step, lambda peer, j: sum_copy(step, peer, j).start()))
 
-    @pl.when(has_down)
-    def _():
-        for copy in to_up:
-            copy.wait_recv()
-        for c in range(nch):
-            prepare(far_x, c * n, fx2, c * n, False, n)
-
-    @pl.when(has_up)
-    def _():
-        for copy in to_down:
-            copy.wait_recv()
-        for c in range(nch):
-            prepare(far_y, c * n, fy2, c * n, True, n)
-
     def totals(group):
         step = 0 if group == 1 else 1
         per_peer(step, lambda peer, j: sum_arrival(group, peer).wait_recv())
@@ -286,29 +278,51 @@
         return jnp.sqrt(total[3:4] * n / total[2:3])
 
     own = totals(1)
-    state_ref[...] = vector * norm(own)
+    state_v[...] = vector * norm(own)
+    state_out = pltpu.make_async_copy(state_v, state_ref, out_sem.at[6])
+    state_out.start()
     energy_ref[...] = own[0:1] / own[1:2]
     scale = 1.0 / jnp.sqrt(f32(n))
 
-    @pl.when(has_down)
-    def _():
-        kept_up.wait_recv()
-        k = far_kept[0] * norm(totals(0))
-        extend(fx2, k, k.T, lb_ref, scale, nch, n)
-
-    @pl.when(s == 0)
-    def _():
-        lb_ref[...] = jnp.zeros_like(lb_ref)
-
-    @pl.when(has_up)
-    def _():
-        kept_down.wait_recv()
-        k = far_kept[1] * norm(totals(2))
-        extend(fy2, k.T, k, rb_ref, scale, nch, n)
-
-    @pl.when(s == nseg - 1)
-    def _():
-        rb_ref[...] = jnp.zeros_like(rb_ref)
+    def outgoing(side):
+        held_out, ref = ((lb_v, lb_ref), (rb_v, rb_ref))[side]
+        return [
+            pltpu.make_async_copy(
+                held_out.at[pl.ds(start, rows)], ref.at[pl.ds(start, rows)],
+                out_sem.at[3 * side + i],
+            )
+            for i, (start, rows, _) in enumerate(chunks)
+        ]
+
+    def extend_side(side):
+        far, ops, out, copies, arrival = (
+            (far_x, fx2, lb_v, to_up, kept_up),
+            (far_y, fy2, rb_v, to_down, kept_down),
+        )[side]
+        for i, (start, rows, _) in enumerate(chunks):
+            copies[i].wait_recv()
+            for at in range(start, start + rows, n):
+                prepare(far, at, ops, at, side == 1, n)
+            if i == 0:
+                arrival.wait_recv()
+                k = far_kept[side] * norm(totals(2 * side))
+                first, second = (k.T, k) if side else (k, k.T)
+                weight, streams = stationary(first), streamed(second)
+            extend(ops, weight, streams, out, scale, start, rows // n, n)
+            outgoing(side)[i].start()
+
+    def clear(side):
+        out = (lb_v, rb_v)[side]
+        out[...] = jnp.zeros_like(out)
+        for copy in outgoing(side):
+            copy.start()
+
+    even = lax.rem(s, 2) == 0
+    pl.when(s == 0)(lambda: clear(0))
+    pl.when(s == nseg - 1)(lambda: clear(1))
+    pl.when(jnp.logical_and(even, has_up))(lambda: extend_side(1))
+    pl.when(has_down)(lambda: extend_side(0))
+    pl.when(jnp.logical_and(jnp.logical_not(even), has_up))(lambda: extend_side(1))
 
     @pl.when(has_next)
     def _():
@@ -331,6 +345,24 @@
             copy.wait_send()
 
     per_segment(lambda step: per_peer(step, lambda peer, j: sum_copy(step, peer, j).wait_send()))
+    for copy in outgoing(0) + outgoing(1) + [state_out]:
+        copy.wait()
+
+
+def write_out(*refs):
+    sem = refs[6]
+    copies = []
+    for i in range(3):
+        rows = refs[i].shape[0] // 2
+        for at in (0, rows):
+            part = pl.ds(at, rows)
+            copies.append(
+                pltpu.make_async_copy(refs[i].at[part], refs[3 + i].at[part], sem.at[len(copies)])
+            )
+    for copy in copies:
+        copy.start()
+    for copy in copies:
+        copy.wait()
 
 
 def shards(nseg, nblk, two_site, diag_left, diag_right, hop_left, hop_right, sector_sizes, ranks):
@@ -339,7 +371,7 @@
     nch = ndiag + nhop
     smem = pl.BlockSpec(memory_space=pltpu.SMEM)
     vmem = pl.BlockSpec(memory_space=pltpu.VMEM)
-    anywhere = pl.BlockSpec(memory_space=pl.ANY)
+    hbm = pl.BlockSpec(memory_space=pltpu.HBM)
     dma = pltpu.SemaphoreType.DMA
     state, left, right, energy = pl.pallas_call(
         functools.partial(kernel, nseg, nblk, ndiag, nhop, n),
@@ -349,11 +381,14 @@
             jax.ShapeDtypeStruct((nch * n, n), f32),
             jax.ShapeDtypeStruct((1, 1), f32),
         ),
-        in_specs=[smem, smem] + [anywhere] * 5,
-        out_specs=(vmem, vmem, vmem, vmem),
+        in_specs=[smem, smem] + [hbm] * 5,
+        out_specs=(hbm, hbm, hbm, vmem),
         scratch_shapes=[
             pltpu.VMEM((nch * n, n), f32),
             pltpu.VMEM((nch * n, n), f32),
+            pltpu.VMEM((nch * n, n), f32),
+            pltpu.VMEM((nch * n, n), f32),
+            pltpu.VMEM((n, n), f32),
             pltpu.VMEM((nch * n, n), f32),
             pltpu.VMEM((nch * n, n), f32),
             pltpu.VMEM((nch * n, 2 * n), bf16),
@@ -375,15 +410,16 @@
             dma((ITERS,)),
             dma((ITERS,)),
             dma((ITERS,)),
-            dma((4,)),
-            dma((4,)),
+            dma((6,)),
+            dma((6,)),
             dma((2,)),
             dma((2,)),
             dma((3, nblk)),
             dma((3, nblk)),
+            dma((7,)),
         ],
         compiler_params=pltpu.CompilerParams(
-            collective_id=0, has_side_effects=True, vmem_limit_bytes=40 * 1024 * 1024
+            collective_id=0, has_side_effects=True, vmem_limit_bytes=57 * 1024 * 1024
         ),
         name="solve",
     )(
@@ -394,6 +430,15 @@
         hop_left.reshape(nhop * n, n),
         hop_right.reshape(nhop * n, n),
     )
+    state, left, right = pl.pallas_call(
+        write_out,
+        out_shape=tuple(jax.ShapeDtypeStruct(x.shape, f32) for x in (state, left, right)),
+        in_specs=[hbm] * 3,
+        out_specs=(hbm,) * 3,
+        scratch_shapes=[dma((6,))],
+        compiler_params=pltpu.CompilerParams(vmem_limit_bytes=57 * 1024 * 1024),
+        name="write_out",
+    )(state, left, right)
     return (
         state.reshape(1, 1, n, n),
         left.reshape(1, 1, nch, n, n),

time: 49.2 us -> 117 us (2.38)
  Pallas kernels: 37.1 us -> 113 us
  local copies, waits for them, and re-layouts: 7.75 us -> 0 us
    pallas_call x0 -> x1, Pallas kernels: none -> 74.6 us  [shards(): pl.pallas_call(write_out, out_shape=tuple((jax.ShapeDtypeStruct(x.shape,...]
    unnamed x13 -> x0, local copies, waits for them, and re-layouts: 7.75 us -> none
    pallas_call x1, Pallas kernels: 37.1 us -> 38.2 us  [shards(): pl.pallas_call(functools.partial(kernel, nseg, nblk, ndiag, nhop, n), out...]
where the time goes in v2:
time: 117 us
  Pallas kernels  113 us (97%)
  between operations  3.68 us (3%)
    pallas_call x1, Pallas kernels, shards(): pl.pallas_call(write_out, out_shape=tuple((jax.ShapeDtypeStruct(x.shape,...  74.6 us
    pallas_call x1, Pallas kernels, shards(): pl.pallas_call(functools.partial(kernel, nseg, nblk, ndiag, nhop, n), out...  38.2 us

profile of v2, /device:TPU:1, one launch (start us, length us, event | category | flops | bytes accessed | tf_op | source)
XLA Modules:
  0.0 116.5 jit_solution(908030953524685528)
XLA Ops:
  1.9 38.2 %solve.1 = (f32[128,128]{1,0:T(8,128)}, f32[2304,128]{1,0:T(8,128)}, f32[2304,128]{1,0:T(8,128)}, f32[1,1]{1,0:T(1,128)}) custom-call(s32[1,1]{1,0:T(1,128)S(6)} %copy.12.size_ref, s32[1,1]{1,0:T(1,128)S(6)} %copy.13.rank_ref, f32[128,128]{1,0:T(8,128)} %bitcast.13, f32[256,128]{1,0:T(8,128)} %bitcast.11, f32[256,128]{1,0:T(8,128)} %bitcast.12, ...), custom_call_target="tpu_custom_call" | custom-call | tf_op jit(solution)/shard_map/solve/pallas_call | solution.py:376
  40.2 74.6 %write_out.1 = (f32[128,128]{1,0:T(8,128)}, f32[2304,128]{1,0:T(8,128)}, f32[2304,128]{1,0:T(8,128)}) custom-call(f32[128,128]{1,0:T(8,128)} %get-tuple-element.11.refs_0_, f32[2304,128]{1,0:T(8,128)} %get-tuple-element.12.refs_1_, f32[2304,128]{1,0:T(8,128)} %get-tuple-element.13.refs_2_), custom_call_target="tpu_custom_call" | custom-call | tf_op jit(solution)/shard_map/write_out/pallas_call | solution.py:433

commit v3 on v2

--- a/solution.py
+++ b/solution.py
@@ -82,7 +82,7 @@
     state_ref, lb_ref, rb_ref, energy_ref,
     xl, yr, far_x, far_y, state_v, lb_v, rb_v, a2, at2, b2, bt2, fx2, fy2, held,
     v_buf, c_buf, rv, rc, kept, far_kept, sums,
-    load_sem, v_send, v_recv, c_send, c_recv, x_send, x_recv, k_send, k_recv, s_send, s_recv, out_sem,
+    load_sem, v_send, v_recv, c_send, c_recv, x_send, x_recv, k_send, k_recv, s_send, s_recv, out_sem, relay, r_send, r_recv,
 ):
     s = lax.axis_index("seg")
     q = lax.axis_index("blk")
@@ -128,6 +128,23 @@
 
     per_segment(greet)
 
+    below, above = nseg // 2 - 1, nseg // 2
+    relays = ((below, nseg - 1, above), (above, 0, below))
+
+    def on_relay(action):
+        for origin, via, target in relays:
+            action(origin, via, target)
+
+    def greet_relay(origin, via, target):
+        for first, second in ((origin, via), (via, origin), (via, target), (target, via)):
+            @pl.when(s == first)
+            def _(second=second):
+                pl.semaphore_signal(
+                    barrier, inc=1, device_id={"seg": second, "blk": q}, device_id_type=MESH
+                )
+
+    on_relay(greet_relay)
+
     @pl.when(q == 0)
     def _():
         rv[...] = jnp.zeros_like(rv)
@@ -147,7 +164,10 @@
     v_buf[0] = live * c_buf[ITERS]
 
     groups = 1 + jnp.minimum(s, 1) + jnp.minimum(nseg - 1 - s, 1)
-    pl.semaphore_wait(barrier, groups * nblk - 1)
+    others = 0
+    for place in (0, below, above, nseg - 1):
+        others = others + 2 * (1 - jnp.minimum(jnp.maximum(s - place, place - s), 1))
+    pl.semaphore_wait(barrier, groups * nblk - 1 + others)
 
     def remote(src, dst, send, recv, where):
         return pltpu.make_async_remote_copy(
@@ -185,15 +205,36 @@
 
     pl.when(has_next)(lambda: send_v(0).start())
 
-    @pl.when(has_up)
-    def _():
-        for copy in to_up:
-            copy.start()
-
-    @pl.when(has_down)
-    def _():
-        for copy in to_down:
-            copy.start()
+    def to_relay(origin, via, target):
+        start, rows, _ = chunks[1]
+        source = hl_ref if origin < target else hr_ref
+        return remote(
+            source.at[pl.ds(start - small, rows)], relay, r_send.at[0], r_recv.at[0],
+            {"seg": via, "blk": q},
+        )
+
+    def from_relay(origin, via, target):
+        start, rows, _ = chunks[1]
+        far, i = (far_x, 1) if origin < target else (far_y, 4)
+        return remote(
+            relay, far.at[pl.ds(start, rows)], r_send.at[1], x_recv.at[i],
+            {"seg": target, "blk": q},
+        )
+
+    def send_environments(action):
+        on_relay(lambda *way: pl.when(s == way[0])(lambda: action(to_relay(*way))))
+        for copies, some, middle in ((to_up, has_up, below), (to_down, has_down, above)):
+            pl.when(some)(lambda: action(copies[0]))
+            pl.when(jnp.logical_and(some, s != middle))(lambda: action(copies[1]))
+            pl.when(some)(lambda: action(copies[2]))
+
+    def pass_on(*way):
+        @pl.when(s == way[1])
+        def _():
+            to_relay(*way).wait_recv()
+            from_relay(*way).start()
+
+    send_environments(lambda copy: copy.start())
 
     loads[1].wait()
     loads[2].wait()
@@ -231,6 +272,7 @@
         carried(k)
         finish(k)
         pl.when(has_next)(lambda: send_v(k + 1).start())
+        pl.when(k == 1)(lambda: on_relay(pass_on))
         return carry
 
     lax.fori_loop(1, ITERS - 1, middle, 0)
@@ -334,35 +376,37 @@
         for k in range(ITERS):
             send_c(k).wait_send()
 
-    @pl.when(has_up)
-    def _():
-        for copy in to_up + [kept_up]:
-            copy.wait_send()
-
-    @pl.when(has_down)
-    def _():
-        for copy in to_down + [kept_down]:
-            copy.wait_send()
-
+    send_environments(lambda copy: copy.wait_send())
+    on_relay(lambda *way: pl.when(s == way[1])(lambda: from_relay(*way).wait_send()))
+    pl.when(has_up)(lambda: kept_up.wait_send())
+    pl.when(has_down)(lambda: kept_down.wait_send())
     per_segment(lambda step: per_peer(step, lambda peer, j: sum_copy(step, peer, j).wait_send()))
     for copy in outgoing(0) + outgoing(1) + [state_out]:
         copy.wait()
 
 
 def write_out(*refs):
-    sem = refs[6]
+    loaded, sems = refs[6:9], refs[9]
     copies = []
     for i in range(3):
-        rows = refs[i].shape[0] // 2
-        for at in (0, rows):
-            part = pl.ds(at, rows)
+        rows = refs[i].shape[0]
+        step = max(rows // 3, 128)
+        for at in range(0, rows, step):
+            part = pl.ds(at, min(step, rows - at))
+            j = len(copies)
             copies.append(
-                pltpu.make_async_copy(refs[i].at[part], refs[3 + i].at[part], sem.at[len(copies)])
+                (
+                    pltpu.make_async_copy(refs[i].at[part], loaded[i].at[part], sems.at[0, j]),
+                    pltpu.make_async_copy(loaded[i].at[part], refs[3 + i].at[part], sems.at[1, j]),
+                )
             )
-    for copy in copies:
-        copy.start()
-    for copy in copies:
-        copy.wait()
+    for load, _ in copies:
+        load.start()
+    for load, store in copies:
+        load.wait()
+        store.start()
+    for _, store in copies:
+        store.wait()
 
 
 def shards(nseg, nblk, two_site, diag_left, diag_right, hop_left, hop_right, sector_sizes, ranks):
@@ -417,6 +461,9 @@
             dma((3, nblk)),
             dma((3, nblk)),
             dma((7,)),
+            pltpu.VMEM((nhop * n - nhop // 2 * n, n), f32),
+            dma((2,)),
+            dma((1,)),
         ],
         compiler_params=pltpu.CompilerParams(
             collective_id=0, has_side_effects=True, vmem_limit_bytes=57 * 1024 * 1024
@@ -435,7 +482,7 @@
         out_shape=tuple(jax.ShapeDtypeStruct(x.shape, f32) for x in (state, left, right)),
         in_specs=[hbm] * 3,
         out_specs=(hbm,) * 3,
-        scratch_shapes=[dma((6,))],
+        scratch_shapes=[pltpu.VMEM(x.shape, f32) for x in (state, left, right)] + [dma((2, 8))],
         compiler_params=pltpu.CompilerParams(vmem_limit_bytes=57 * 1024 * 1024),
         name="write_out",
     )(state, left, right)

time: 117 us -> 39.4 us (0.34)
  Pallas kernels: 113 us -> 35.6 us
    pallas_call x1, Pallas kernels: 74.6 us -> 2.57 us  [shards(): pl.pallas_call(write_out, out_shape=tuple((jax.ShapeDtypeStruct(x.shape,...]
    pallas_call x1, Pallas kernels: 38.2 us -> 33 us  [shards(): pl.pallas_call(functools.partial(kernel, nseg, nblk, ndiag, nhop, n), out...]
where the time goes in v3:
time: 39.4 us; the launch traced here: 39.2 us
  Pallas kernels  35.6 us (90%)
  between operations  3.68 us (9%)
    pallas_call x1, Pallas kernels, shards(): pl.pallas_call(functools.partial(kernel, nseg, nblk, ndiag, nhop, n), out...  33 us
    pallas_call x1, Pallas kernels, shards(): pl.pallas_call(write_out, out_shape=tuple((jax.ShapeDtypeStruct(x.shape,...  2.57 us

profile of v3, /device:TPU:1, one launch (start us, length us, event | category | flops | bytes accessed | tf_op | source)
XLA Modules:
  0.0 39.2 jit_solution(1680264972843251189)
XLA Ops:
  1.9 33.0 %solve.1 = (f32[128,128]{1,0:T(8,128)}, f32[2304,128]{1,0:T(8,128)}, f32[2304,128]{1,0:T(8,128)}, f32[1,1]{1,0:T(1,128)}) custom-call(s32[1,1]{1,0:T(1,128)S(6)} %copy.12.size_ref, s32[1,1]{1,0:T(1,128)S(6)} %copy.13.rank_ref, f32[128,128]{1,0:T(8,128)} %bitcast.13, f32[256,128]{1,0:T(8,128)} %bitcast.11, f32[256,128]{1,0:T(8,128)} %bitcast.12, ...), custom_call_target="tpu_custom_call" | custom-call | tf_op jit(solution)/shard_map/solve/pallas_call | solution.py:420
  34.9 2.6 %write_out.1 = (f32[128,128]{1,0:T(8,128)}, f32[2304,128]{1,0:T(8,128)}, f32[2304,128]{1,0:T(8,128)}) custom-call(f32[128,128]{1,0:T(8,128)} %get-tuple-element.11.refs_0_, f32[2304,128]{1,0:T(8,128)} %get-tuple-element.12.refs_1_, f32[2304,128]{1,0:T(8,128)} %get-tuple-element.13.refs_2_), custom_call_target="tpu_custom_call" | custom-call | tf_op jit(solution)/shard_map/write_out/pallas_call | solution.py:480

commit v4 on v3

--- a/solution.py
+++ b/solution.py
@@ -163,6 +163,13 @@
     loads[0].wait()
     v_buf[0] = live * c_buf[ITERS]
 
+    loads[1].wait()
+    loads[2].wait()
+    for h in range(nhop):
+        at = small + h * n
+        prepare(xl, at, at2, h * n, True, n)
+        prepare(yr, at, b2, h * n, False, n)
+
     groups = 1 + jnp.minimum(s, 1) + jnp.minimum(nseg - 1 - s, 1)
     others = 0
     for place in (0, below, above, nseg - 1):
@@ -235,13 +242,6 @@
             from_relay(*way).start()
 
     send_environments(lambda copy: copy.start())
-
-    loads[1].wait()
-    loads[2].wait()
-    for h in range(nhop):
-        at = small + h * n
-        prepare(xl, at, at2, h * n, True, n)
-        prepare(yr, at, b2, h * n, False, n)
 
     def carried(k):
         first_stage(at2, 0, nhop, stationary(v_buf[k]), held, 0, n)
@@ -268,6 +268,17 @@
     finish(0)
     pl.when(has_next)(lambda: send_v(1).start())
 
+    sides = ((far_x, fx2, lb_v, to_up, kept_up), (far_y, fy2, rb_v, to_down, kept_down))
+    even = lax.rem(s, 2) == 0
+    odd = jnp.logical_not(even)
+
+    def prepare_side(side):
+        far, ops, _, copies, _ = sides[side]
+        for copy in copies:
+            copy.wait_recv()
+        for c in range(nch):
+            prepare(far, c * n, ops, c * n, side == 1, n)
+
     def middle(k, carry):
         carried(k)
         finish(k)
@@ -277,6 +288,8 @@
 
     lax.fori_loop(1, ITERS - 1, middle, 0)
     carried(ITERS - 1)
+    pl.when(jnp.logical_and(even, has_up))(lambda: prepare_side(1))
+    pl.when(jnp.logical_and(odd, has_down))(lambda: prepare_side(0))
     applied, vector = finish(ITERS - 1)
     last = v_buf[ITERS - 1]
     kept[...] = vector * col_live
@@ -307,6 +320,9 @@
         )
 
     per_segment(lambda step: per_peer(step, lambda peer, j: sum_copy(step, peer, j).start()))
+
+    pl.when(jnp.logical_and(even, has_down))(lambda: prepare_side(0))
+    pl.when(jnp.logical_and(odd, has_up))(lambda: prepare_side(1))
 
     def totals(group):
         step = 0 if group == 1 else 1
@@ -337,19 +353,12 @@
         ]
 
     def extend_side(side):
-        far, ops, out, copies, arrival = (
-            (far_x, fx2, lb_v, to_up, kept_up),
-            (far_y, fy2, rb_v, to_down, kept_down),
-        )[side]
+        _, ops, out, _, arrival = sides[side]
+        arrival.wait_recv()
+        k = far_kept[side] * norm(totals(2 * side))
+        first, second = (k.T, k) if side else (k, k.T)
+        weight, streams = stationary(first), streamed(second)
         for i, (start, rows, _) in enumerate(chunks):
-            copies[i].wait_recv()
-            for at in range(start, start + rows, n):
-                prepare(far, at, ops, at, side == 1, n)
-            if i == 0:
-                arrival.wait_recv()
-                k = far_kept[side] * norm(totals(2 * side))
-                first, second = (k.T, k) if side else (k, k.T)
-                weight, streams = stationary(first), streamed(second)
             extend(ops, weight, streams, out, scale, start, rows // n, n)
             outgoing(side)[i].start()
 
@@ -359,12 +368,11 @@
         for copy in outgoing(side):
             copy.start()
 
-    even = lax.rem(s, 2) == 0
     pl.when(s == 0)(lambda: clear(0))
     pl.when(s == nseg - 1)(lambda: clear(1))
     pl.when(jnp.logical_and(even, has_up))(lambda: extend_side(1))
     pl.when(has_down)(lambda: extend_side(0))
-    pl.when(jnp.logical_and(jnp.logical_not(even), has_up))(lambda: extend_side(1))
+    pl.when(jnp.logical_and(odd, has_up))(lambda: extend_side(1))
 
     @pl.when(has_next)
     def _():
@@ -385,8 +393,10 @@
         copy.wait()
 
 
-def write_out(*refs):
-    loaded, sems = refs[6:9], refs[9]
+def write_out(energy_ref, state_ref, left_ref, right_ref, energy_out, state_out, left_out, right_out, *rest):
+    refs = (state_ref, left_ref, right_ref, state_out, left_out, right_out)
+    loaded, sems = rest[0:3], rest[3]
+    energy_out[...] = energy_ref[...]
     copies = []
     for i in range(3):
         rows = refs[i].shape[0]
@@ -477,15 +487,15 @@
         hop_left.reshape(nhop * n, n),
         hop_right.reshape(nhop * n, n),
     )
-    state, left, right = pl.pallas_call(
+    energy, state, left, right = pl.pallas_call(
         write_out,
-        out_shape=tuple(jax.ShapeDtypeStruct(x.shape, f32) for x in (state, left, right)),
-        in_specs=[hbm] * 3,
-        out_specs=(hbm,) * 3,
+        out_shape=tuple(jax.ShapeDtypeStruct(x.shape, f32) for x in (energy, state, left, right)),
+        in_specs=[vmem] + [hbm] * 3,
+        out_specs=(vmem,) + (hbm,) * 3,
         scratch_shapes=[pltpu.VMEM(x.shape, f32) for x in (state, left, right)] + [dma((2, 8))],
         compiler_params=pltpu.CompilerParams(vmem_limit_bytes=57 * 1024 * 1024),
         name="write_out",
-    )(state, left, right)
+    )(energy, state, left, right)
     return (
         state.reshape(1, 1, n, n),
         left.reshape(1, 1, nch, n, n),

time: 39.4 us -> 39 us (0.990)
  between operations: 3.68 us -> 1.93 us
  Pallas kernels: 35.6 us -> 36.9 us
    pallas_call x1, Pallas kernels: 2.57 us -> 3.7 us  [shards(): pl.pallas_call(write_out, out_shape=tuple((jax.ShapeDtypeStruct(x.shape,...]
where the time goes in v4:
time: 39 us; the launch traced here: 38.8 us
  Pallas kernels  36.9 us (95%)
  between operations  1.93 us (5%)
    pallas_call x1, Pallas kernels, shards(): pl.pallas_call(functools.partial(kernel, nseg, nblk, ndiag, nhop, n), out...  33.2 us
    pallas_call x1, Pallas kernels, shards(): pl.pallas_call(write_out, out_shape=tuple((jax.ShapeDtypeStruct(x.shape,...  3.7 us

profile of v4, /device:TPU:1, one launch (start us, length us, event | category | flops | bytes accessed | tf_op | source)
XLA Modules:
  0.0 38.8 jit_solution(16651124916017802564)
XLA Ops:
  1.9 33.2 %solve.1 = (f32[128,128]{1,0:T(8,128)}, f32[2304,128]{1,0:T(8,128)}, f32[2304,128]{1,0:T(8,128)}, f32[1,1]{1,0:T(1,128)}) custom-call(s32[1,1]{1,0:T(1,128)S(6)} %copy.11.size_ref, s32[1,1]{1,0:T(1,128)S(6)} %copy.12.rank_ref, f32[128,128]{1,0:T(8,128)} %bitcast.13, f32[256,128]{1,0:T(8,128)} %bitcast.11, f32[256,128]{1,0:T(8,128)} %bitcast.12, ...), custom_call_target="tpu_custom_call" | custom-call | tf_op jit(solution)/shard_map/solve/pallas_call | solution.py:430
  35.1 3.7 %write_out.1 = (f32[1,1]{1,0:T(1,128)}, f32[128,128]{1,0:T(8,128)}, f32[2304,128]{1,0:T(8,128)}, f32[2304,128]{1,0:T(8,128)}) custom-call(f32[1,1]{1,0:T(1,128)} %get-tuple-element.12.energy_ref, f32[128,128]{1,0:T(8,128)} %get-tuple-element.13.state_ref, f32[2304,128]{1,0:T(8,128)} %get-tuple-element.14.left_ref, f32[2304,128]{1,0:T(8,128)} %get-tuple-element.15.right_ref), custom_call_target="tpu_custom_call" | custom-call | tf_op jit(solution)/shard_map/write_out/pallas_call | solution.py:490

commit v5 on v4

--- a/solution.py
+++ b/solution.py
@@ -8,7 +8,7 @@
 from jax.sharding import PartitionSpec as P
 
 ITERS = 4
-BATCH = 8
+BATCH = 4
 MESH = pl.DeviceIdType.MESH
 f32 = jnp.float32
 bf16 = jnp.bfloat16
@@ -47,20 +47,32 @@
 
 
 def first_stage(ops, start, count, weight, held, column, n):
-    for c in range(0, count, BATCH):
-        size = min(BATCH, count - c)
-        got = dot(ops[start + c * n : start + (c + size) * n, :], weight)
-        got = got[:, 0:n] + got[:, n : 2 * n]
-        hi, lo = split(got)
-        for part in range(size):
-            lanes = column + (c + part) * n
-            held[0:n, lanes : lanes + n] = hi[part * n : (part + 1) * n]
-            held[n : 2 * n, lanes : lanes + n] = lo[part * n : (part + 1) * n]
+    got = dot(ops[start : start + count * n, :], weight)
+    got = got[:, 0:n] + got[:, n : 2 * n]
+    hi, lo = split(got)
+    for c in range(count):
+        lanes = column + c * n
+        held[0:n, lanes : lanes + n] = hi[c * n : (c + 1) * n]
+        held[n : 2 * n, lanes : lanes + n] = lo[c * n : (c + 1) * n]
 
 
 def second_stage(held, column, count, ops, start, n):
     got = dot(held[:, column : column + count * n], ops[start : start + count * n, :])
     return (got[0:n, 0:n] + got[0:n, n : 2 * n]) + (got[n : 2 * n, 0:n] + got[n : 2 * n, n : 2 * n])
+
+
+def both_stages(left, right, start, count, weight, held, n):
+    total, waiting = None, None
+    for c in list(range(0, count, BATCH)) + [None]:
+        if c is not None:
+            size = min(BATCH, count - c)
+            first_stage(left, start + c * n, size, weight, held, start + c * n, n)
+        if waiting is not None:
+            at, some = waiting
+            term = second_stage(held, at, some, right, at, n)
+            total = term if total is None else total + term
+        waiting = None if c is None else (start + c * n, size)
+    return total
 
 
 def extend(ops, weight, rows, out, scale, start, count, n):
@@ -163,13 +175,6 @@
     loads[0].wait()
     v_buf[0] = live * c_buf[ITERS]
 
-    loads[1].wait()
-    loads[2].wait()
-    for h in range(nhop):
-        at = small + h * n
-        prepare(xl, at, at2, h * n, True, n)
-        prepare(yr, at, b2, h * n, False, n)
-
     groups = 1 + jnp.minimum(s, 1) + jnp.minimum(nseg - 1 - s, 1)
     others = 0
     for place in (0, below, above, nseg - 1):
@@ -243,16 +248,21 @@
 
     send_environments(lambda copy: copy.start())
 
+    loads[1].wait()
+    loads[2].wait()
+    for h in range(nhop):
+        at = small + h * n
+        prepare(xl, at, at2, h * n, True, n)
+        prepare(yr, at, b2, h * n, False, n)
+
     def carried(k):
-        first_stage(at2, 0, nhop, stationary(v_buf[k]), held, 0, n)
-        c_buf[k] = second_stage(held, 0, nhop, b2, 0, n)
+        c_buf[k] = both_stages(at2, b2, 0, nhop, stationary(v_buf[k]), held, n)
         pl.when(has_previous)(lambda: send_c(k).start())
 
     def finish(k):
-        first_stage(a2, 0, ndiag, stationary(v_buf[k]), held, 0, n)
+        own = both_stages(a2, bt2, 0, ndiag, stationary(v_buf[k]), held, n)
         pl.when(has_previous)(lambda: send_v(k).wait_recv())
-        first_stage(a2, small, nhop, stationary(rv[k]), held, small, n)
-        own = second_stage(held, 0, nch, bt2, 0, n)
+        own = own + both_stages(a2, bt2, small, nhop, stationary(rv[k]), held, n)
         pl.when(has_next)(lambda: send_c(k).wait_recv())
         applied = live * (own + rc[k])
         vector = spectral_shift * v_buf[k] - applied
@@ -393,21 +403,21 @@
         copy.wait()
 
 
-def write_out(energy_ref, state_ref, left_ref, right_ref, energy_out, state_out, left_out, right_out, *rest):
-    refs = (state_ref, left_ref, right_ref, state_out, left_out, right_out)
-    loaded, sems = rest[0:3], rest[3]
-    energy_out[...] = energy_ref[...]
+def write_out(*refs):
+    loaded, sems = refs[8:12], refs[12]
     copies = []
-    for i in range(3):
+    for i in range(4):
         rows = refs[i].shape[0]
         step = max(rows // 3, 128)
         for at in range(0, rows, step):
-            part = pl.ds(at, min(step, rows - at))
+            size = min(step, rows - at)
             j = len(copies)
+            part = (lambda ref: ref) if size == rows else (lambda ref: ref.at[pl.ds(at, size)])
+            source, middle, target = part(refs[i]), part(loaded[i]), part(refs[4 + i])
             copies.append(
                 (
-                    pltpu.make_async_copy(refs[i].at[part], loaded[i].at[part], sems.at[0, j]),
-                    pltpu.make_async_copy(loaded[i].at[part], refs[3 + i].at[part], sems.at[1, j]),
+                    pltpu.make_async_copy(source, middle, sems.at[0, j]),
+                    pltpu.make_async_copy(middle, target, sems.at[1, j]),
                 )
             )
     for load, _ in copies:
@@ -490,9 +500,10 @@
     energy, state, left, right = pl.pallas_call(
         write_out,
         out_shape=tuple(jax.ShapeDtypeStruct(x.shape, f32) for x in (energy, state, left, right)),
-        in_specs=[vmem] + [hbm] * 3,
-        out_specs=(vmem,) + (hbm,) * 3,
-        scratch_shapes=[pltpu.VMEM(x.shape, f32) for x in (state, left, right)] + [dma((2, 8))],
+        in_specs=[hbm] * 4,
+        out_specs=(hbm,) * 4,
+        scratch_shapes=[pltpu.VMEM(x.shape, f32) for x in (energy, state, left, right)]
+        + [dma((2, 8))],
         compiler_params=pltpu.CompilerParams(vmem_limit_bytes=57 * 1024 * 1024),
         name="write_out",
     )(energy, state, left, right)

time: 39 us -> 38.5 us (0.987)
  Pallas kernels: 36.9 us -> 36.4 us
    pallas_call x1, Pallas kernels: 3.7 us -> 3.19 us  [shards(): pl.pallas_call(write_out, out_shape=tuple((jax.ShapeDtypeStruct(x.shape,...]
where the time goes in v5:
time: 38.5 us; the launch traced here: 38.3 us
  Pallas kernels  36.4 us (95%)
  between operations  1.93 us (5%)
    pallas_call x1, Pallas kernels, shards(): pl.pallas_call(functools.partial(kernel, nseg, nblk, ndiag, nhop, n), out...  33.2 us
    pallas_call x1, Pallas kernels, shards(): pl.pallas_call(write_out, out_shape=tuple((jax.ShapeDtypeStruct(x.shape,...  3.19 us

profile of v5, /device:TPU:1, one launch (start us, length us, event | category | flops | bytes accessed | tf_op | source)
XLA Modules:
  0.0 38.3 jit_solution(14323241940040194235)
XLA Ops:
  1.9 33.2 %solve.1 = (f32[128,128]{1,0:T(8,128)}, f32[2304,128]{1,0:T(8,128)}, f32[2304,128]{1,0:T(8,128)}, f32[1,1]{1,0:T(1,128)}) custom-call(s32[1,1]{1,0:T(1,128)S(6)} %copy.11.size_ref, s32[1,1]{1,0:T(1,128)S(6)} %copy.12.rank_ref, f32[128,128]{1,0:T(8,128)} %bitcast.13, f32[256,128]{1,0:T(8,128)} %bitcast.11, f32[256,128]{1,0:T(8,128)} %bitcast.12, ...), custom_call_target="tpu_custom_call" | custom-call | tf_op jit(solution)/shard_map/solve/pallas_call | solution.py:440
  35.1 3.2 %write_out.1 = (f32[1,1]{1,0:T(1,128)}, f32[128,128]{1,0:T(8,128)}, f32[2304,128]{1,0:T(8,128)}, f32[2304,128]{1,0:T(8,128)}) custom-call(f32[1,1]{1,0:T(1,128)} %get-tuple-element.12.refs_0_, f32[128,128]{1,0:T(8,128)} %get-tuple-element.13.refs_1_, f32[2304,128]{1,0:T(8,128)} %get-tuple-element.14.refs_2_, f32[2304,128]{1,0:T(8,128)} %get-tuple-element.15.refs_3_), custom_call_target="tpu_custom_call" | custom-call | tf_op jit(solution)/shard_map/write_out/pallas_call | solution.py:500

commit v6 on v5

--- a/solution.py
+++ b/solution.py
@@ -194,7 +194,7 @@
         return remote(c_buf.at[k], rc.at[k], c_send.at[k], c_recv.at[k], {"seg": s, "blk": q - 1})
 
     up, down = {"seg": s + 1, "blk": q}, {"seg": s - 1, "blk": q}
-    half = nhop // 2 * n
+    half = (nhop // 2 - 1) * n
     chunks = [(small, half, 1), (small + half, nhop * n - half, 1), (0, small, 0)]
 
     def environment(refs, far, first, where):
@@ -282,12 +282,16 @@
     even = lax.rem(s, 2) == 0
     odd = jnp.logical_not(even)
 
+    def prepare_chunk(side, i):
+        far, ops, _, copies, _ = sides[side]
+        start, rows, _ = chunks[i]
+        copies[i].wait_recv()
+        for at in range(start, start + rows, n):
+            prepare(far, at, ops, at, side == 1, n)
+
     def prepare_side(side):
-        far, ops, _, copies, _ = sides[side]
-        for copy in copies:
-            copy.wait_recv()
-        for c in range(nch):
-            prepare(far, c * n, ops, c * n, side == 1, n)
+        for i in range(len(chunks)):
+            prepare_chunk(side, i)
 
     def middle(k, carry):
         carried(k)
@@ -331,8 +335,8 @@
 
     per_segment(lambda step: per_peer(step, lambda peer, j: sum_copy(step, peer, j).start()))
 
-    pl.when(jnp.logical_and(even, has_down))(lambda: prepare_side(0))
-    pl.when(jnp.logical_and(odd, has_up))(lambda: prepare_side(1))
+    pl.when(jnp.logical_and(even, has_down))(lambda: prepare_chunk(0, 0))
+    pl.when(jnp.logical_and(odd, has_up))(lambda: prepare_chunk(1, 0))
 
     def totals(group):
         step = 0 if group == 1 else 1
@@ -362,13 +366,15 @@
             for i, (start, rows, _) in enumerate(chunks)
         ]
 
-    def extend_side(side):
+    def extend_side(side, late):
         _, ops, out, _, arrival = sides[side]
         arrival.wait_recv()
         k = far_kept[side] * norm(totals(2 * side))
         first, second = (k.T, k) if side else (k, k.T)
         weight, streams = stationary(first), streamed(second)
         for i, (start, rows, _) in enumerate(chunks):
+            if late and i > 0:
+                prepare_chunk(side, i)
             extend(ops, weight, streams, out, scale, start, rows // n, n)
             outgoing(side)[i].start()
 
@@ -380,9 +386,10 @@
 
     pl.when(s == 0)(lambda: clear(0))
     pl.when(s == nseg - 1)(lambda: clear(1))
-    pl.when(jnp.logical_and(even, has_up))(lambda: extend_side(1))
-    pl.when(has_down)(lambda: extend_side(0))
-    pl.when(jnp.logical_and(odd, has_up))(lambda: extend_side(1))
+    pl.when(jnp.logical_and(even, has_up))(lambda: extend_side(1, False))
+    pl.when(jnp.logical_and(odd, has_down))(lambda: extend_side(0, False))
+    pl.when(jnp.logical_and(even, has_down))(lambda: extend_side(0, True))
+    pl.when(jnp.logical_and(odd, has_up))(lambda: extend_side(1, True))
 
     @pl.when(has_next)
     def _():
@@ -481,7 +488,7 @@
             dma((3, nblk)),
             dma((3, nblk)),
             dma((7,)),
-            pltpu.VMEM((nhop * n - nhop // 2 * n, n), f32),
+            pltpu.VMEM((nhop * n - (nhop // 2 - 1) * n, n), f32),
             dma((2,)),
             dma((1,)),
         ],
@@ -497,16 +504,16 @@
         hop_left.reshape(nhop * n, n),
         hop_right.reshape(nhop * n, n),
     )
-    energy, state, left, right = pl.pallas_call(
+    left, right, state, energy = pl.pallas_call(
         write_out,
-        out_shape=tuple(jax.ShapeDtypeStruct(x.shape, f32) for x in (energy, state, left, right)),
+        out_shape=tuple(jax.ShapeDtypeStruct(x.shape, f32) for x in (left, right, state, energy)),
         in_specs=[hbm] * 4,
         out_specs=(hbm,) * 4,
-        scratch_shapes=[pltpu.VMEM(x.shape, f32) for x in (energy, state, left, right)]
+        scratch_shapes=[pltpu.VMEM(x.shape, f32) for x in (left, right, state, energy)]
         + [dma((2, 8))],
         compiler_params=pltpu.CompilerParams(vmem_limit_bytes=57 * 1024 * 1024),
         name="write_out",
-    )(energy, state, left, right)
+    )(left, right, state, energy)
     return (
         state.reshape(1, 1, n, n),
         left.reshape(1, 1, nch, n, n),

time: 38.5 us -> 37.6 us (0.977)
  Pallas kernels: 36.4 us -> 35.5 us
    pallas_call x1, Pallas kernels: 33.2 us -> 32.3 us  [shards(): pl.pallas_call(functools.partial(kernel, nseg, nblk, ndiag, nhop, n), out...]
where the time goes in v6:
time: 37.6 us; the launch traced here: 37.4 us
  Pallas kernels  35.5 us (94%)
  between operations  1.93 us (5%)
    pallas_call x1, Pallas kernels, shards(): pl.pallas_call(functools.partial(kernel, nseg, nblk, ndiag, nhop, n), out...  32.3 us
    pallas_call x1, Pallas kernels, shards(): pl.pallas_call(write_out, out_shape=tuple((jax.ShapeDtypeStruct(x.shape,...  3.16 us

profile of v6, /device:TPU:1, one launch (start us, length us, event | category | flops | bytes accessed | tf_op | source)
XLA Modules:
  0.0 37.4 jit_solution(4789189474780462499)
XLA Ops:
  1.9 32.3 %solve.1 = (f32[128,128]{1,0:T(8,128)}, f32[2304,128]{1,0:T(8,128)}, f32[2304,128]{1,0:T(8,128)}, f32[1,1]{1,0:T(1,128)}) custom-call(s32[1,1]{1,0:T(1,128)S(6)} %copy.11.size_ref, s32[1,1]{1,0:T(1,128)S(6)} %copy.12.rank_ref, f32[128,128]{1,0:T(8,128)} %bitcast.13, f32[256,128]{1,0:T(8,128)} %bitcast.11, f32[256,128]{1,0:T(8,128)} %bitcast.12, ...), custom_call_target="tpu_custom_call" | custom-call | tf_op jit(solution)/shard_map/solve/pallas_call | solution.py:447
  34.3 3.2 %write_out.1 = (f32[2304,128]{1,0:T(8,128)}, f32[2304,128]{1,0:T(8,128)}, f32[128,128]{1,0:T(8,128)}, f32[1,1]{1,0:T(1,128)}) custom-call(f32[2304,128]{1,0:T(8,128)} %get-tuple-element.12.refs_0_, f32[2304,128]{1,0:T(8,128)} %get-tuple-element.13.refs_1_, f32[128,128]{1,0:T(8,128)} %get-tuple-element.14.refs_2_, f32[1,1]{1,0:T(1,128)} %get-tuple-element.15.refs_3_), custom_call_target="tpu_custom_call" | custom-call | tf_op jit(solution)/shard_map/write_out/pallas_call | solution.py:507

commit v7 on v6

--- a/solution.py
+++ b/solution.py
@@ -194,7 +194,7 @@
         return remote(c_buf.at[k], rc.at[k], c_send.at[k], c_recv.at[k], {"seg": s, "blk": q - 1})
 
     up, down = {"seg": s + 1, "blk": q}, {"seg": s - 1, "blk": q}
-    half = (nhop // 2 - 1) * n
+    half = (nhop // 2 - 2) * n
     chunks = [(small, half, 1), (small + half, nhop * n - half, 1), (0, small, 0)]
 
     def environment(refs, far, first, where):
@@ -335,9 +335,6 @@
 
     per_segment(lambda step: per_peer(step, lambda peer, j: sum_copy(step, peer, j).start()))
 
-    pl.when(jnp.logical_and(even, has_down))(lambda: prepare_chunk(0, 0))
-    pl.when(jnp.logical_and(odd, has_up))(lambda: prepare_chunk(1, 0))
-
     def totals(group):
         step = 0 if group == 1 else 1
         per_peer(step, lambda peer, j: sum_arrival(group, peer).wait_recv())
@@ -373,7 +370,7 @@
         first, second = (k.T, k) if side else (k, k.T)
         weight, streams = stationary(first), streamed(second)
         for i, (start, rows, _) in enumerate(chunks):
-            if late and i > 0:
+            if late:
                 prepare_chunk(side, i)
             extend(ops, weight, streams, out, scale, start, rows // n, n)
             outgoing(side)[i].start()
@@ -488,7 +485,7 @@
             dma((3, nblk)),
             dma((3, nblk)),
             dma((7,)),
-            pltpu.VMEM((nhop * n - (nhop // 2 - 1) * n, n), f32),
+            pltpu.VMEM((nhop * n - (nhop // 2 - 2) * n, n), f32),
             dma((2,)),
             dma((1,)),
         ],

time: 37.6 us -> 36.9 us (0.981)
  Pallas kernels: 35.5 us -> 34.8 us
    pallas_call x1, Pallas kernels: 32.3 us -> 31.7 us  [shards(): pl.pallas_call(functools.partial(kernel, nseg, nblk, ndiag, nhop, n), out...]
where the time goes in v7:
time: 36.9 us; the launch traced here: 36.7 us
  Pallas kernels  34.8 us (94%)
  between operations  1.93 us (5%)
    pallas_call x1, Pallas kernels, shards(): pl.pallas_call(functools.partial(kernel, nseg, nblk, ndiag, nhop, n), out...  31.7 us
    pallas_call x1, Pallas kernels, shards(): pl.pallas_call(write_out, out_shape=tuple((jax.ShapeDtypeStruct(x.shape,...  3.16 us

profile of v7, /device:TPU:1, one launch (start us, length us, event | category | flops | bytes accessed | tf_op | source)
XLA Modules:
  0.0 36.7 jit_solution(6642860208817140174)
XLA Ops:
  1.9 31.7 %solve.1 = (f32[128,128]{1,0:T(8,128)}, f32[2304,128]{1,0:T(8,128)}, f32[2304,128]{1,0:T(8,128)}, f32[1,1]{1,0:T(1,128)}) custom-call(s32[1,1]{1,0:T(1,128)S(6)} %copy.11.size_ref, s32[1,1]{1,0:T(1,128)S(6)} %copy.12.rank_ref, f32[128,128]{1,0:T(8,128)} %bitcast.13, f32[256,128]{1,0:T(8,128)} %bitcast.11, f32[256,128]{1,0:T(8,128)} %bitcast.12, ...), custom_call_target="tpu_custom_call" | custom-call | tf_op jit(solution)/shard_map/solve/pallas_call | solution.py:444
  33.6 3.2 %write_out.1 = (f32[2304,128]{1,0:T(8,128)}, f32[2304,128]{1,0:T(8,128)}, f32[128,128]{1,0:T(8,128)}, f32[1,1]{1,0:T(1,128)}) custom-call(f32[2304,128]{1,0:T(8,128)} %get-tuple-element.12.refs_0_, f32[2304,128]{1,0:T(8,128)} %get-tuple-element.13.refs_1_, f32[128,128]{1,0:T(8,128)} %get-tuple-element.14.refs_2_, f32[1,1]{1,0:T(1,128)} %get-tuple-element.15.refs_3_), custom_call_target="tpu_custom_call" | custom-call | tf_op jit(solution)/shard_map/write_out/pallas_call | solution.py:504
